TPU v7x, 512 devices: a whole 4x4x16 slice. The times are simulated.
512 devices in a mesh: dp: 64 (over x, z), mp: 8 (over y, core).
Axes of the slice: x: 4, y: 4, z: 16, core: 2. Of those that a mesh axis runs over, the one named last changes fastest.
Arguments:
- resp_q: bfloat16 [64, 128, 8192], P('dp', None, 'mp'), may hold values from -12 to 12, as said below
- resp_kv: bfloat16 [2, 64, 128, 1024], P(None, 'dp', None, 'mp'), may hold values from -4 to 4
- d_out: bfloat16 [64, 128, 8192], P('dp', None, 'mp'), may hold values from -6 to 6
- lengths: int32 [64], P('dp'), may hold values from 1 to 128, 6144 in all
- fork: int32 [64], replicated, may hold values from 0 to 127
- page_table: int32 [128, 32], replicated, may hold values from 0 to 4095, as said below
- pool_pages: bfloat16 [4096, 2, 16, 1024], P(('dp', 'mp')), may hold values from -4 to 4
- pool_scales: bfloat16 [4096, 2, 8], P(('dp', 'mp')), may hold values from 0.29882812 to 3
Outputs:
- d_query: bfloat16 [64, 128, 8192], P('dp', None, 'mp')
- d_resp_kv: bfloat16 [2, 64, 128, 1024], P(None, 'dp', None, 'mp')
- d_pool: float32 [4096, 2, 16, 1024], P(('dp', 'mp'))
Inputs may be any that keep to these rules, and one draw needn't show every extreme that they name: `page_table`: every pool page is named exactly once. Pool page g lies on dp index g // 64, and the 32 pages of one prompt lie on 32 different dp indices. `resp_q`: query entries. On some rows, some query heads may be a multiple between 1.5 and 3 of a key of the same response, so that scores can reach several hundred.
All inputs are finite; a program needn't handle non-finite values. No bound on the sum of `lengths` on one device may be relied on, other than what follows from the above.
Results may differ from a plain program's by a relative error of at most 0.012.
Values may be sent and summed in bfloat16 or wider, within the bound.
No kernel may reach another device: no remote copies, remote signals or barrier semaphores. Data moves between devices by JAX's collectives and lax.ppermute only.
A program may use at most 64 MiB of HBM per device.

v0:
```python
import jax
import jax.numpy as jnp
from jax import lax
from jax.sharding import PartitionSpec as P

DH = 128


def dequantize(stored, factors):
    heads = factors.shape[-1]
    head_width = stored.shape[-1] // heads
    shaped = stored.astype(jnp.float32).reshape(
        stored.shape[0], 2, stored.shape[2], heads, head_width
    )
    scaled = shaped * factors.astype(jnp.float32).reshape(stored.shape[0], 2, 1, heads, 1)
    return scaled.astype(jnp.bfloat16).reshape(stored.shape)


def per_device(resp_q, resp_kv, d_out, lengths, fork, page_table, pool_pages, pool_scales):
    dp_size = lax.axis_size("dp")
    mp_size = lax.axis_size("mp")
    my_dp = lax.axis_index("dp")
    pool_dev = pool_pages.shape[0]
    heads_kv = pool_scales.shape[-1]
    kv_dev = heads_kv // mp_size
    page_rows = pool_pages.shape[2]
    pages_prompt = page_table.shape[1]
    prompt_len = pages_prompt * page_rows
    resp_len = resp_q.shape[1]
    total = prompt_len + resp_len
    group_rows = mp_size * pool_dev
    inv_root = 1.0 / DH**0.5
    regrouped, regscales = (
        lax.all_to_all(pool_pages, "mp", split_axis=3, concat_axis=0, tiled=True),
        lax.all_to_all(
            pool_scales.reshape(pool_dev, 2, 1, heads_kv),
            "mp",
            split_axis=3,
            concat_axis=0,
            tiled=True,
        ),
    )
    wanted = jnp.take(page_table, fork, axis=0)
    on_device = wanted // group_rows == my_dp
    send_rows = jnp.sum(jnp.where(on_device, wanted % group_rows, 0), axis=1)
    has_page = jnp.any(on_device, axis=1)
    my_pages = jnp.take(wanted, my_dp, axis=0)
    sources = my_pages // group_rows
    arrived, arrived_scales = (
        lax.all_to_all(
            jnp.take(regrouped, send_rows, axis=0), "dp", split_axis=0, concat_axis=0, tiled=True
        ),
        lax.all_to_all(
            jnp.take(regscales, send_rows, axis=0), "dp", split_axis=0, concat_axis=0, tiled=True
        ),
    )
    prompt_pages = dequantize(
        jnp.take(arrived, sources, axis=0), jnp.take(arrived_scales, sources, axis=0)
    )
    key_all = jnp.concatenate(
        [prompt_pages[:, 0].reshape(prompt_len, kv_dev * DH), resp_kv[0, 0]], 0
    )
    value_all = jnp.concatenate(
        [prompt_pages[:, 1].reshape(prompt_len, kv_dev * DH), resp_kv[1, 0]], 0
    )
    key_heads = key_all.reshape(total, kv_dev, DH).transpose(1, 0, 2)
    value_heads = value_all.reshape(total, kv_dev, DH).transpose(1, 0, 2)
    heads_q_dev = resp_q.shape[2] // DH
    group_size = heads_q_dev // kv_dev
    blocks = heads_q_dev // 2
    rows_live = jnp.arange(resp_len) < lengths[0]
    grad_masked = jnp.where(rows_live[:, None], d_out[0], jnp.zeros_like(d_out[0]))
    query_blocks = (
        resp_q[0]
        .reshape(resp_len, blocks, 2, DH)
        .transpose(1, 2, 0, 3)
        .reshape(blocks, 2 * resp_len, DH)
    )
    grad_blocks = (
        grad_masked.reshape(resp_len, blocks, 2, DH)
        .transpose(1, 2, 0, 3)
        .reshape(blocks, 2 * resp_len, DH)
    )
    kv_index = jnp.arange(blocks) * 2 // group_size
    positions = jnp.tile(jnp.arange(resp_len), 2)
    key_cols = jnp.arange(total)
    allowed = (key_cols[None, :] < prompt_len) | (
        key_cols[None, :] - prompt_len <= positions[:, None]
    )
    across = (((1,), (1,)), ((), ()))
    down = (((0,), (0,)), ((), ()))

    def block_step(block_items):
        q_rows, g_rows, kv_slot = block_items
        k_head = key_heads[kv_slot]
        v_head = value_heads[kv_slot]
        scores = (
            lax.dot_general(q_rows, k_head, across, preferred_element_type=jnp.float32) * inv_root
        )
        scores = jnp.where(allowed, scores, -1e30)
        row_max = jnp.max(scores, axis=-1, keepdims=True)
        exp_scores = jnp.exp(scores - row_max)
        weights = exp_scores / jnp.sum(exp_scores, axis=-1, keepdims=True)
        weights_b = weights.astype(jnp.bfloat16)
        attn_out = jnp.dot(weights_b, v_head, preferred_element_type=jnp.float32)
        row_delta = jnp.sum(g_rows.astype(jnp.float32) * attn_out, axis=-1)
        grad_weights = lax.dot_general(g_rows, v_head, across, preferred_element_type=jnp.float32)
        grad_scores = (weights * (grad_weights - row_delta[:, None])).astype(jnp.bfloat16)
        grad_query = (
            jnp.dot(grad_scores, k_head, preferred_element_type=jnp.float32) * inv_root
        ).astype(jnp.bfloat16)
        grad_keys = (
            lax.dot_general(grad_scores, q_rows, down, preferred_element_type=jnp.float32)
            * inv_root
        )
        grad_values = lax.dot_general(weights_b, g_rows, down, preferred_element_type=jnp.float32)
        return (grad_query, grad_keys, grad_values)

    query_parts, key_parts, value_parts = lax.map(block_step, (query_blocks, grad_blocks, kv_index))
    key_sum = key_parts.reshape(kv_dev, group_size // 2, total, DH).sum(axis=1)
    value_sum = value_parts.reshape(kv_dev, group_size // 2, total, DH).sum(axis=1)
    d_query = (
        query_parts.reshape(blocks, 2, resp_len, DH)
        .transpose(2, 0, 1, 3)
        .reshape(1, resp_len, heads_q_dev * DH)
    )
    own_grads = jnp.stack([key_sum[:, prompt_len:], value_sum[:, prompt_len:]])
    own_grads = (
        own_grads.transpose(0, 2, 1, 3).reshape(2, 1, resp_len, kv_dev * DH).astype(jnp.bfloat16)
    )
    prompt_grad = jnp.stack([key_sum[:, :prompt_len], value_sum[:, :prompt_len]])
    prompt_grad = prompt_grad.reshape(2, kv_dev, pages_prompt, page_rows, DH).transpose(
        2, 0, 3, 1, 4
    )
    prompt_grad = prompt_grad.reshape(pages_prompt, 2, page_rows, kv_dev * DH)
    buffer = (
        jnp.zeros((dp_size, 2, page_rows, kv_dev * DH), jnp.float32).at[sources].set(prompt_grad)
    )
    returned = lax.all_to_all(buffer, "dp", split_axis=0, concat_axis=0, tiled=True)
    select = ((send_rows[:, None] == jnp.arange(group_rows)[None, :]) & has_page[:, None]).astype(
        jnp.float32
    )
    summed = jnp.einsum("hn,hxyz->nxyz", select, returned, precision=lax.Precision.HIGHEST)
    restored = lax.all_to_all(summed, "mp", split_axis=0, concat_axis=3, tiled=True)
    return (d_query, own_grads, restored)


def solution(mesh):
    return jax.shard_map(
        per_device,
        mesh=mesh,
        in_specs=(
            P("dp", None, "mp"),
            P(None, "dp", None, "mp"),
            P("dp", None, "mp"),
            P("dp"),
            P(),
            P(),
            P(("dp", "mp"), None, None, None),
            P(("dp", "mp"), None, None),
        ),
        out_specs=(
            P("dp", None, "mp"),
            P(None, "dp", None, "mp"),
            P(("dp", "mp"), None, None, None),
        ),
        check_vma=False,
    )
```

profile of v0, /device:TPU:1, one launch (start us, length us, event | category | flops | bytes accessed | tf_op | source)
XLA Modules:
  0.0 215.1 jit_solution(4193142531082206402)
XLA Ops:
  0.6 1.4 copy.73
  2.0 10.1 %all-to-all-start.2 = ((bf16[8,2,1,8]{0,1,2,3:T(2,128)(2,1)}), bf16[8,2,1,8]{0,1,2,3:T(2,128)(2,1)S(1)}, u32[]{:S(2)}, u32[]{:S(2)}) async-start(bf16[8,2,1,8]{0,1,2,3:T(2,128)(2,1)} %copy.73), calls=%async_computation.2 | async-start | bytes 8192 | tf_op jit(solution)/shard_map/all_to_all | solution.py:35
  15.2 5.7 %copy.69 = bf16[8,2,16,1024]{2,0,1,3:T(8,128)(2,1)} copy(bf16[8,2,16,1024]{3,2,1,0:T(8,128)(2,1)} %param.16) | data formatting | bytes 1048576 | tf_op args[6]
  20.9 6.5 %reshape.354 = bf16[8,2,16384]{2,1,0:T(2,128)(2,1)} reshape(bf16[1024,2,8,16]{3,2,1,0:T(8,128)(2,1)} %bitcast.158) | data formatting | bytes 1048576
  27.3 4.8 %all-to-all-start = ((bf16[8,2,16384]{2,1,0:T(2,128)(2,1)}), bf16[8,2,16384]{2,1,0:T(2,128)(2,1)S(1)}, u32[]{:S(2)}, u32[]{:S(2)}) async-start(bf16[8,2,16384]{2,1,0:T(2,128)(2,1)} %reshape.354), calls=%async_computation | async-start | bytes 1048576 | tf_op jit(solution)/shard_map/all_to_all | solution.py:34
  33.9 7.7 %all-to-all-done = bf16[8,2,16384]{2,1,0:T(2,128)(2,1)S(1)} async-done(((bf16[8,2,16384]{2,1,0:T(2,128)(2,1)}), bf16[8,2,16384]{2,1,0:T(2,128)(2,1)S(1)}, u32[]{:S(2)}, u32[]{:S(2)}) %all-to-all-start) | async-done | bytes 524320 | tf_op jit(solution)/shard_map/all_to_all | solution.py:34
  41.6 14.1 %all-to-all-start.3 = ((bf16[64,2,1,1]{1,3,2,0:T(2,128)(2,1)}), bf16[64,2,1,1]{1,3,2,0:T(2,128)(2,1)S(1)}, u32[]{:S(2)}, u32[]{:S(2)}) async-start(bf16[64,2,1,1]{1,3,2,0:T(2,128)(2,1)} %copy.78), calls=%async_computation.3 | async-start | bytes 65536 | tf_op jit(solution)/shard_map/all_to_all | solution.py:53
  55.8 4.1 %reshape.355 = bf16[1024,2,8,16]{3,2,1,0:T(8,128)(2,1)} reshape(bf16[8,2,16384]{2,1,0:T(2,128)(2,1)S(1)} %all-to-all-done) | data formatting | bytes 1048576
  59.9 4.7 %copy.71 = bf16[8,8,2,16,128]{4,3,2,1,0:T(8,128)(2,1)S(1)} copy(bf16[8,8,2,16,128]{3,1,2,4,0:T(8,128)(2,1)} %bitcast.157) | data formatting | bytes 1048576 | tf_op jit(solution)/shard_map/all_to_all | solution.py:34
  66.3 2.7 %all-to-all-done.3 = bf16[64,2,1,1]{1,3,2,0:T(2,128)(2,1)S(1)} async-done(((bf16[64,2,1,1]{1,3,2,0:T(2,128)(2,1)}), bf16[64,2,1,1]{1,3,2,0:T(2,128)(2,1)S(1)}, u32[]{:S(2)}, u32[]{:S(2)}) %all-to-all-start.3) | async-done | bytes 288 | tf_op jit(solution)/shard_map/all_to_all | solution.py:53
  69.0 12.1 %all-to-all-start.1 = ((bf16[64,2,16,128]{3,2,1,0:T(8,128)(2,1)}), bf16[64,2,16,128]{3,2,1,0:T(8,128)(2,1)}, u32[]{:S(2)}, u32[]{:S(2)}) async-start(bf16[64,2,16,128]{3,2,1,0:T(8,128)(2,1)} %broadcast_select_fusion), calls=%async_computation.1 | async-start | bytes 1048576 | tf_op jit(solution)/shard_map/all_to_all | solution.py:50
  86.6 22.9 %all-to-all-done.1 = bf16[64,2,16,128]{3,2,1,0:T(8,128)(2,1)} async-done(((bf16[64,2,16,128]{3,2,1,0:T(8,128)(2,1)}), bf16[64,2,16,128]{3,2,1,0:T(8,128)(2,1)}, u32[]{:S(2)}, u32[]{:S(2)}) %all-to-all-start.1) | async-done | bytes 524320 | tf_op jit(solution)/shard_map/all_to_all | solution.py:50
  109.5 1.6 gather_fusion.2
  111.4 14.7 %while.17 = (s32[]{:T(128)}, bf16[4,256,128]{2,1,0:T(8,128)(2,1)}, f32[4,640,128]{2,1,0:T(8,128)S(1)}, f32[4,640,128]{2,1,0:T(8,128)S(1)}, bf16[4,256,128]{2,1,0...) while((s32[]{:T(128)}, bf16[4,256,128]{2,1,0:T(8,128)(2,1)}, ...), condition=%wide.region_5.6_spmd.clone, body=%wide.region_1.5_spmd.clone.sunk | while | flops 254852352 | bytes 5983489 | solution.py:119
  111.4 1.1 fusion.84
  115.1 1.0 fusion.84
  127.2 1.5 scatter_fusion
  128.7 59.5 %all_to_all.69 = f32[64,2,16,128]{3,2,1,0:T(8,128)S(1)} all-to-all(f32[64,2,16,128]{3,2,1,0:T(8,128)S(1)} %scatter_fusion), channel_id=1, replica_groups=mesh['dp'=64,'mp'=8] {'dp'}, dimensions={0} | all-to-all | bytes 2097152 | tf_op jit(solution)/shard_map/all_to_all | solution.py:139
  188.3 1.3 fusion.34
  189.6 1.6 copy.85
  191.2 7.7 %all-to-all-start.5 = ((f32[64,2,16,128]{3,2,1,0:T(8,128)}), f32[64,2,16,128]{3,2,1,0:T(8,128)S(1)}, u32[]{:S(2)}, u32[]{:S(2)}) async-start(f32[64,2,16,128]{3,2,1,0:T(8,128)} %copy.85), calls=%async_computation.5 | async-start | bytes 2097152 | tf_op jit(solution)/shard_map/all_to_all | solution.py:144
  198.9 1.2 copy.100
  202.5 11.5 %all-to-all-done.5 = f32[64,2,16,128]{3,2,1,0:T(8,128)S(1)} async-done(((f32[64,2,16,128]{3,2,1,0:T(8,128)}), f32[64,2,16,128]{3,2,1,0:T(8,128)S(1)}, u32[]{:S(2)}, u32[]{:S(2)}) %all-to-all-start.5) | async-done | bytes 1048608 | tf_op jit(solution)/shard_map/all_to_all | solution.py:144
  214.0 1.1 copy.99
  (92 shorter events, 27.2 us)
Async XLA Ops:
  2.0 25.3 %all-to-all-start.2 = ((bf16[8,2,1,8]{0,1,2,3:T(2,128)(2,1)}), bf16[8,2,1,8]{0,1,2,3:T(2,128)(2,1)S(1)}, u32[]{:S(2)}, u32[]{:S(2)}) async-start(bf16[8,2,1,8]{0,1,2,3:T(2,128)(2,1)} %copy.73), calls=%async_computation.2 | async-start | bytes 8192 | tf_op jit(solution)/shard_map/all_to_all | solution.py:35
  15.1 17.0 %copy-start.4 = (s32[64]{0:T(128)}, s32[64]{0:T(128)S(1)}, u32[]{:S(2)}) copy-start(s32[64]{0:T(128)S(1)} %fusion.39) | copy-start | bytes 772
  27.3 14.3 %all-to-all-start = ((bf16[8,2,16384]{2,1,0:T(2,128)(2,1)}), bf16[8,2,16384]{2,1,0:T(2,128)(2,1)S(1)}, u32[]{:S(2)}, u32[]{:S(2)}) async-start(bf16[8,2,16384]{2,1,0:T(2,128)(2,1)} %reshape.354), calls=%async_computation | async-start | bytes 1048576 | tf_op jit(solution)/shard_map/all_to_all | solution.py:34
  41.6 27.4 %all-to-all-start.3 = ((bf16[64,2,1,1]{1,3,2,0:T(2,128)(2,1)}), bf16[64,2,1,1]{1,3,2,0:T(2,128)(2,1)S(1)}, u32[]{:S(2)}, u32[]{:S(2)}) async-start(bf16[64,2,1,1]{1,3,2,0:T(2,128)(2,1)} %copy.78), calls=%async_computation.3 | async-start | bytes 65536 | tf_op jit(solution)/shard_map/all_to_all | solution.py:53
  65.3 15.8 %copy-start.1 = (bf16[1,128,1024]{2,1,0:T(8,128)(2,1)S(1)}, bf16[1,128,1024]{2,1,0:T(8,128)(2,1)}, u32[]{:S(2)}) copy-start(bf16[1,128,1024]{2,1,0:T(8,128)(2,1)} %param.12) | copy-start | bytes 786436
  69.0 40.5 %all-to-all-start.1 = ((bf16[64,2,16,128]{3,2,1,0:T(8,128)(2,1)}), bf16[64,2,16,128]{3,2,1,0:T(8,128)(2,1)}, u32[]{:S(2)}, u32[]{:S(2)}) async-start(bf16[64,2,16,128]{3,2,1,0:T(8,128)(2,1)} %broadcast_select_fusion), calls=%async_computation.1 | async-start | bytes 1048576 | tf_op jit(solution)/shard_map/all_to_all | solution.py:50
  81.1 2.4 %copy-start.2 = (bf16[1,128,1024]{2,1,0:T(8,128)(2,1)S(1)}, bf16[1,128,1024]{2,1,0:T(8,128)(2,1)}, u32[]{:S(2)}) copy-start(bf16[1,128,1024]{2,1,0:T(8,128)(2,1)} %param.10) | copy-start | bytes 786436
  83.7 27.6 %copy-start.3 = (bf16[4,256,128]{1,2,0:T(8,128)(2,1)S(1)}, bf16[4,256,128]{1,2,0:T(8,128)(2,1)}, u32[]{:S(2)}) copy-start(bf16[4,256,128]{1,2,0:T(8,128)(2,1)} %reshape.255) | copy-start | bytes 786436
  126.3 0.7 copy-start
  128.7 59.6 %copy-start.5 = (s32[64]{0:T(128)S(1)}, s32[64]{0:T(128)}, u32[]{:S(2)}) copy-start(s32[64]{0:T(128)} %copy-done.4) | copy-start | bytes 772
  191.2 22.9 %all-to-all-start.5 = ((f32[64,2,16,128]{3,2,1,0:T(8,128)}), f32[64,2,16,128]{3,2,1,0:T(8,128)S(1)}, u32[]{:S(2)}, u32[]{:S(2)}) async-start(f32[64,2,16,128]{3,2,1,0:T(8,128)} %copy.85), calls=%async_computation.5 | async-start | bytes 2097152 | tf_op jit(solution)/shard_map/all_to_all | solution.py:144
where the time goes:
time: 216 us; the launch traced here: 215 us
  blocking collectives  59.5 us (28%)
  starting transfers between devices  48.9 us (23%)
  waiting for transfers between devices  44.9 us (21%)
  local copies, waits for them, and re-layouts  39.6 us (18%)
  matrix products  14.8 us (7%)
  other arithmetic  5.58 us (3%)
    all_to_all x1, blocking collectives, per_device(): lax.all_to_all(buffer, 'dp', split_axis=0, concat_axis=0, tiled=True)  59.5 us
    all_to_all x1, waiting for transfers between devices, per_device(): lax.all_to_all(jnp.take(regrouped, send_rows, axis=0), 'dp', split_axis=0...  22.9 us
    unnamed x16, local copies, waits for them, and re-layouts  17.8 us
    all_to_all x1, starting transfers between devices, per_device(): lax.all_to_all(jnp.take(regscales, send_rows, axis=0), 'dp', split_axis=0...  14.1 us
    all_to_all x1, starting transfers between devices, per_device(): lax.all_to_all(jnp.take(regrouped, send_rows, axis=0), 'dp', split_axis=0...  12.1 us
    all_to_all x1, waiting for transfers between devices, per_device(): lax.all_to_all(summed, 'mp', split_axis=0, concat_axis=3, tiled=True)  11.5 us
    all_to_all x1, starting transfers between devices, per_device(): lax.all_to_all(pool_scales.reshape(pool_dev, 2, 1, heads_kv), 'mp', split...  10.1 us
    all_to_all x1, starting transfers between devices, per_device(): lax.all_to_all(summed, 'mp', split_axis=0, concat_axis=3, tiled=True)  7.74 us
  transfers between devices with their start and end apart: 5, of which 4 were waited for; matrix products, arithmetic and copies ran while one was open for 17% of the time, Pallas kernels for 0%

commit v1 on v0

v1 whole, which is shorter than its diff:
```python
import functools
import math

import jax
import jax.numpy as jnp
from jax import lax
from jax.experimental import pallas as pl
from jax.experimental.pallas import tpu as pltpu
from jax.sharding import PartitionSpec as P

DH = 128
SMEM = pl.BlockSpec(memory_space=pltpu.SMEM)
VMEM = pl.BlockSpec(memory_space=pltpu.VMEM)
PARAMS = pltpu.CompilerParams(vmem_limit_bytes=48 * 1024 * 1024)


def scale_kernel(pages_ref, scales_ref, out_ref):
    rows = pages_ref.shape[0]
    heads = scales_ref.shape[1]
    factors = scales_ref[...].astype(jnp.float32)
    repeat = rows // factors.shape[0]
    factors = jnp.broadcast_to(factors[:, None, :], (factors.shape[0], repeat, heads))
    factors = factors.reshape(rows, heads)
    for j in range(heads):
        stored = pages_ref[:, j * DH : (j + 1) * DH].astype(jnp.float32)
        out_ref[j] = (stored * factors[:, j : j + 1]).astype(jnp.bfloat16)


def select_kernel(rows_ref, pages_ref, out_ref):
    for r in range(out_ref.shape[0]):
        out_ref[r] = pages_ref[rows_ref[r]]


def attention_kernel(
    page_rows,
    sources_ref,
    length_ref,
    arrived_ref,
    own_ref,
    q_ref,
    g_ref,
    d_query_ref,
    d_own_ref,
    sent_ref,
    key_ref,
    value_ref,
):
    pages = sources_ref.shape[0]
    prompt_len = pages * page_rows
    resp_len = q_ref.shape[0]
    heads = q_ref.shape[1] // DH
    per_block = 2
    width = per_block * resp_len
    inv_root = 1.0 / DH**0.5
    to_exp2 = inv_root * math.log2(math.e)
    for i in range(pages):
        slot = sources_ref[i]
        key_ref[i * page_rows : (i + 1) * page_rows] = arrived_ref[slot, :page_rows]
        value_ref[i * page_rows : (i + 1) * page_rows] = arrived_ref[slot, page_rows:]
    key_ref[prompt_len:] = own_ref[0]
    value_ref[prompt_len:] = own_ref[1]
    keys = key_ref[...]
    values = value_ref[...]
    keys_t = keys.astype(jnp.float32).T.astype(jnp.bfloat16)
    live = lax.broadcasted_iota(jnp.int32, (resp_len, DH), 0) < length_ref[0]
    across = (((1,), (1,)), ((), ()))
    own_pos = lax.broadcasted_iota(jnp.int32, (resp_len, width), 0)
    row_pos = lax.broadcasted_iota(jnp.int32, (resp_len, width), 1) % resp_len
    allowed = own_pos <= row_pos
    key_grad = None
    value_grad = None
    for b in range(heads // per_block):
        cols = [slice((b * per_block + k) * DH, (b * per_block + k + 1) * DH) for k in range(per_block)]
        q = jnp.concatenate([q_ref[:, c] for c in cols], axis=0)
        g = jnp.concatenate([jnp.where(live, g_ref[:, c], jnp.zeros_like(g_ref[:, c])) for c in cols], axis=0)
        scores = lax.dot_general(keys, q, across, preferred_element_type=jnp.float32) * to_exp2
        prompt_scores = scores[:prompt_len]
        own_scores = jnp.where(allowed, scores[prompt_len:], -1e30)
        top = jnp.maximum(
            jnp.max(prompt_scores, axis=0, keepdims=True), jnp.max(own_scores, axis=0, keepdims=True)
        )
        exps = jnp.exp2(jnp.concatenate([prompt_scores, own_scores], axis=0) - top)
        weights = exps * (1.0 / jnp.sum(exps, axis=0, keepdims=True))
        weights_b = weights.astype(jnp.bfloat16)
        grad_weights = lax.dot_general(values, g, across, preferred_element_type=jnp.float32)
        delta = jnp.sum(weights_b.astype(jnp.float32) * grad_weights, axis=0, keepdims=True)
        grad_scores = (weights * (grad_weights - delta)).astype(jnp.bfloat16)
        part = jnp.dot(weights_b, g, preferred_element_type=jnp.float32)
        value_grad = part if value_grad is None else value_grad + part
        part = jnp.dot(grad_scores, q, preferred_element_type=jnp.float32)
        key_grad = part if key_grad is None else key_grad + part
        d_q = jnp.dot(keys_t, grad_scores, preferred_element_type=jnp.float32) * inv_root
        for k, c in enumerate(cols):
            d_query_ref[:, c] = d_q[:, k * resp_len : (k + 1) * resp_len].T.astype(jnp.bfloat16)
    key_grad = (key_grad * inv_root).astype(jnp.bfloat16)
    value_grad = value_grad.astype(jnp.bfloat16)
    d_own_ref[0] = key_grad[prompt_len:]
    d_own_ref[1] = value_grad[prompt_len:]
    for i in range(pages):
        slot = sources_ref[i]
        sent_ref[slot, :page_rows] = key_grad[i * page_rows : (i + 1) * page_rows]
        sent_ref[slot, page_rows:] = value_grad[i * page_rows : (i + 1) * page_rows]


def sum_kernel(rows_ref, arrived_ref, out_ref, total_ref):
    pages = out_ref.shape[0]
    total_ref[...] = jnp.zeros_like(total_ref)
    for r in range(arrived_ref.shape[0]):
        row = rows_ref[r]
        total_ref[row] = total_ref[row] + arrived_ref[r].astype(jnp.float32)
    out_ref[...] = total_ref[:pages].astype(jnp.bfloat16)


def layout_kernel(parts_ref, out_ref):
    for j in range(parts_ref.shape[0]):
        out_ref[:, j * DH : (j + 1) * DH] = parts_ref[j].astype(jnp.float32)


def per_device(resp_q, resp_kv, d_out, lengths, fork, page_table, pool_pages, pool_scales):
    dp_size = lax.axis_size("dp")
    mp_size = lax.axis_size("mp")
    my_dp = lax.axis_index("dp")
    pool_dev, _, page_rows, _ = pool_pages.shape
    heads_kv = pool_scales.shape[-1]
    pages_prompt = page_table.shape[1]
    resp_len = resp_q.shape[1]
    total = pages_prompt * page_rows + resp_len
    group_rows = mp_size * pool_dev
    slot_rows = 2 * page_rows
    bf16 = jnp.bfloat16

    by_head = pl.pallas_call(
        scale_kernel,
        out_shape=jax.ShapeDtypeStruct((heads_kv, pool_dev * slot_rows, DH), bf16),
        in_specs=[VMEM, VMEM],
        out_specs=VMEM,
        compiler_params=PARAMS,
    )(pool_pages.reshape(pool_dev * slot_rows, -1), pool_scales.reshape(pool_dev * 2, heads_kv))
    regrouped = lax.all_to_all(by_head, "mp", split_axis=0, concat_axis=0, tiled=True)
    regrouped = regrouped.reshape(group_rows, slot_rows, DH)

    wanted = jnp.take(page_table, fork, axis=0)
    on_device = wanted // group_rows == my_dp
    send_rows = jnp.sum(jnp.where(on_device, wanted % group_rows, 0), axis=1)
    sum_rows = jnp.where(jnp.any(on_device, axis=1), send_rows, group_rows)
    sources = jnp.take(wanted, my_dp, axis=0) // group_rows

    slots = jax.ShapeDtypeStruct((dp_size, slot_rows, DH), bf16)
    selected = pl.pallas_call(
        select_kernel,
        out_shape=slots,
        in_specs=[SMEM, VMEM],
        out_specs=VMEM,
        compiler_params=PARAMS,
    )(send_rows, regrouped)
    arrived = lax.all_to_all(selected, "dp", split_axis=0, concat_axis=0, tiled=True)

    d_query, d_own, sent = pl.pallas_call(
        functools.partial(attention_kernel, page_rows),
        out_shape=(
            jax.ShapeDtypeStruct(resp_q.shape[1:], bf16),
            jax.ShapeDtypeStruct((2, resp_len, DH), bf16),
            slots,
        ),
        in_specs=[SMEM, SMEM, VMEM, VMEM, VMEM, VMEM],
        out_specs=(VMEM, VMEM, VMEM),
        scratch_shapes=[pltpu.VMEM((total, DH), bf16), pltpu.VMEM((total, DH), bf16)],
        compiler_params=PARAMS,
    )(sources, lengths, arrived, resp_kv[:, 0], resp_q[0], d_out[0])

    returned = lax.all_to_all(sent, "dp", split_axis=0, concat_axis=0, tiled=True)
    summed = pl.pallas_call(
        sum_kernel,
        out_shape=jax.ShapeDtypeStruct((group_rows, slot_rows, DH), bf16),
        in_specs=[SMEM, VMEM],
        out_specs=VMEM,
        scratch_shapes=[pltpu.VMEM((group_rows + 1, slot_rows, DH), jnp.float32)],
        compiler_params=PARAMS,
    )(sum_rows, returned)
    restored = lax.all_to_all(
        summed.reshape(mp_size, pool_dev * slot_rows, DH), "mp", split_axis=0, concat_axis=0, tiled=True
    )
    d_pool = pl.pallas_call(
        layout_kernel,
        out_shape=jax.ShapeDtypeStruct((pool_dev * slot_rows, heads_kv * DH), jnp.float32),
        in_specs=[VMEM],
        out_specs=VMEM,
        compiler_params=PARAMS,
    )(restored)
    return d_query[None], d_own[:, None], d_pool.reshape(pool_pages.shape)


def solution(mesh):
    return jax.shard_map(
        per_device,
        mesh=mesh,
        in_specs=(
            P("dp", None, "mp"),
            P(None, "dp", None, "mp"),
            P("dp", None, "mp"),
            P("dp"),
            P(),
            P(),
            P(("dp", "mp"), None, None, None),
            P(("dp", "mp"), None, None),
        ),
        out_specs=(
            P("dp", None, "mp"),
            P(None, "dp", None, "mp"),
            P(("dp", "mp"), None, None, None),
        ),
        check_vma=False,
    )
```

time: 216 us -> 128 us (0.59)
  blocking collectives: 59.5 us -> 15.2 us
  local copies, waits for them, and re-layouts: 39.6 us -> 3.09 us
  waiting for transfers between devices: 44.9 us -> 65.2 us
  starting transfers between devices: 48.9 us -> 33.4 us
  matrix products: 14.8 us -> 0 us
  Pallas kernels: 0 us -> 9 us
  other arithmetic: 5.58 us -> 0.36 us
    all_to_all x1, blocking collectives: 59.5 us -> 15.2 us  [per_device(): lax.all_to_all(summed.reshape(mp_size, pool_dev * slot_rows, DH), 'mp', s...]
    all_to_all x5 -> x3, waiting for transfers between devices: 44.9 us -> 65.2 us  [the longest x1 29 us: per_device(): lax.all_to_all(sent, 'dp', split_axis=0, concat_axis=0, tiled=True)]
    all_to_all x5 -> x3, starting transfers between devices: 48.9 us -> 33.4 us  [the longest x1 14.1 us: per_device(): lax.all_to_all(selected, 'dp', split_axis=0, concat_axis=0, tiled=True)]
    unnamed x16 -> x15, local copies, waits for them, and re-layouts: 17.8 us -> 2.49 us
    dot_general x25 -> x0, matrix products: 14.8 us -> none  [the longest x4 4.19 us: block_step(): lax.dot_general(q_rows, k_head, across, preferred_element_type=jnp.float32)]
    pallas_call x0 -> x5, Pallas kernels: none -> 9 us  [the longest x1 4.58 us: per_device(): pl.pallas_call(functools.partial(attention_kernel, page_rows), out_shape=...]
    all_to_all x6 -> x0, local copies, waits for them, and re-layouts: 6.26 us -> none  [the longest x1 4.72 us: per_device(): lax.all_to_all(pool_pages, 'mp', split_axis=3, concat_axis=0, tiled=True)]
    reshape x5 -> x0, local copies, waits for them, and re-layouts: 4.37 us -> none  [the longest x1 1.36 us: per_device(): pool_scales.reshape(pool_dev, 2, 1, heads_kv)]
  transfers between devices with their start and end apart: 5 -> 3, of which waited for: 4 -> 3; matrix products, arithmetic and copies ran while one was open for 17% -> 1% of each run, Pallas kernels for 0% -> 0%
where the time goes in v1:
time: 128 us
  waiting for transfers between devices  65.2 us (51%)
  starting transfers between devices  33.4 us (26%)
  blocking collectives  15.2 us (12%)
  Pallas kernels  9 us (7%)
  local copies, waits for them, and re-layouts  3.09 us (2%)
  between operations  1.35 us (1%)
    all_to_all x1, waiting for transfers between devices, per_device(): lax.all_to_all(sent, 'dp', split_axis=0, concat_axis=0, tiled=True)  29 us
    all_to_all x1, waiting for transfers between devices, per_device(): lax.all_to_all(selected, 'dp', split_axis=0, concat_axis=0, tiled=True)  28.4 us
    all_to_all x1, blocking collectives, per_device(): lax.all_to_all(summed.reshape(mp_size, pool_dev * slot_rows, DH), 'mp', s...  15.2 us
    all_to_all x1, starting transfers between devices, per_device(): lax.all_to_all(selected, 'dp', split_axis=0, concat_axis=0, tiled=True)  14.1 us
    all_to_all x1, starting transfers between devices, per_device(): lax.all_to_all(by_head, 'mp', split_axis=0, concat_axis=0, tiled=True)  10.4 us
    all_to_all x1, starting transfers between devices, per_device(): lax.all_to_all(sent, 'dp', split_axis=0, concat_axis=0, tiled=True)  8.94 us
    all_to_all x1, waiting for transfers between devices, per_device(): lax.all_to_all(by_head, 'mp', split_axis=0, concat_axis=0, tiled=True)  7.8 us
    pallas_call x1, Pallas kernels, per_device(): pl.pallas_call(functools.partial(attention_kernel, page_rows), out_shape=...  4.58 us
  transfers between devices with their start and end apart: 3, of which 3 were waited for; matrix products, arithmetic and copies ran while one was open for 1% of the time, Pallas kernels for 0%

profile of v1, /device:TPU:1, one launch (start us, length us, event | category | flops | bytes accessed | tf_op | source)
XLA Modules:
  0.0 127.6 jit_solution(1749286945123605828)
XLA Ops:
  0.6 0.0 copy-start
  0.6 1.0 copy-done
  1.7 0.7 copy-done.4
  2.4 1.0 shard_map.103
  3.4 10.4 %all-to-all-start = ((bf16[8,256,128]{2,1,0:T(8,128)(2,1)}), bf16[8,256,128]{2,1,0:T(8,128)(2,1)S(1)}, u32[]{:S(2)}, u32[]{:S(2)}) async-start(bf16[8,256,128]{2,1,0:T(8,128)(2,1)} %shard_map.103), calls=%async_computation | async-start | bytes 1048576 | tf_op jit(solution)/shard_map/all_to_all | solution.py:139
  13.8 0.7 copy-done.6
  14.5 0.0 copy-done.5
  14.5 0.1 copy.11
  14.6 0.6 gather_fusion
  15.2 0.2 fusion.6
  15.4 0.1 fusion.2.rows_ref
  15.5 7.8 %all-to-all-done = bf16[8,256,128]{2,1,0:T(8,128)(2,1)S(1)} async-done(((bf16[8,256,128]{2,1,0:T(8,128)(2,1)}), bf16[8,256,128]{2,1,0:T(8,128)(2,1)S(1)}, u32[]{:S(2)}, u32[]{:S(2)}) %all-to-all-start) | async-done | bytes 524320 | tf_op jit(solution)/shard_map/all_to_all | solution.py:139
  23.3 1.4 %shard_map.104 = bf16[64,32,128]{2,1,0:T(8,128)(2,1)} custom-call(s32[64]{0:T(128)S(1)} %fusion.2.rows_ref, bf16[64,32,128]{2,1,0:T(8,128)(2,1)S(1)} %bitcast.16), custom_call_target="tpu_custom_call" | custom-call | tf_op jit(solution)/shard_map/pallas_call | solution.py:149
  24.7 14.1 %all-to-all-start.1 = ((bf16[64,32,128]{2,1,0:T(8,128)(2,1)}), bf16[64,32,128]{2,1,0:T(8,128)(2,1)S(1)}, u32[]{:S(2)}, u32[]{:S(2)}) async-start(bf16[64,32,128]{2,1,0:T(8,128)(2,1)} %shard_map.104), calls=%async_computation.1 | async-start | bytes 1048576 | tf_op jit(solution)/shard_map/all_to_all | solution.py:156
  39.4 28.4 %all-to-all-done.1.arrived_ref = bf16[64,32,128]{2,1,0:T(8,128)(2,1)S(1)} async-done(((bf16[64,32,128]{2,1,0:T(8,128)(2,1)}), bf16[64,32,128]{2,1,0:T(8,128)(2,1)S(1)}, u32[]{:S(2)}, u32[]{:S(2)}) %all-to-all-start.1) | async-done | bytes 524320 | tf_op jit(solution)/shard_map/all_to_all | solution.py:156
  67.8 0.0 copy-done.1
  67.8 0.0 copy-done.2
  67.8 0.0 copy-done.3
  67.8 4.6 %shard_map.105 = (bf16[128,1024]{1,0:T(8,128)(2,1)}, bf16[2,128,128]{2,1,0:T(8,128)(2,1)}, bf16[64,32,128]{2,1,0:T(8,128)(2,1)}) custom-call(s32[32]{0:T(128)S(1)} %and_select_fusion.sources_ref, s32[1]{0:T(128)S(6)} %copy.13.length_ref, bf16[64,32,128]{2,1,0:T(8,128)(2,1)S(1)} %all-to-all-done.1.arrived_ref, bf16[2,128,128]{2,1,0:T(8,128)(2,1)S(1)} %bitcast.21, ...), custom_call_target="tpu_custom_call" | custom-call | tf_op jit(solution)/shard_map/pallas_call | solution.py:158
  72.4 8.9 %all-to-all-start.2 = ((bf16[64,32,128]{2,1,0:T(8,128)(2,1)}), bf16[64,32,128]{2,1,0:T(8,128)(2,1)S(1)}, u32[]{:S(2)}, u32[]{:S(2)}) async-start(bf16[64,32,128]{2,1,0:T(8,128)(2,1)} %get-tuple-element.8), calls=%async_computation.2 | async-start | bytes 1048576 | tf_op jit(solution)/shard_map/all_to_all | solution.py:171
  81.4 29.0 %all-to-all-done.2.arrived_ref = bf16[64,32,128]{2,1,0:T(8,128)(2,1)S(1)} async-done(((bf16[64,32,128]{2,1,0:T(8,128)(2,1)}), bf16[64,32,128]{2,1,0:T(8,128)(2,1)S(1)}, u32[]{:S(2)}, u32[]{:S(2)}) %all-to-all-start.2) | async-done | bytes 524320 | tf_op jit(solution)/shard_map/all_to_all | solution.py:171
  110.4 0.9 shard_map.106
  111.3 15.2 %all_to_all.20.parts_ref = bf16[8,256,128]{2,1,0:T(8,128)(2,1)S(1)} all-to-all(bf16[8,256,128]{2,1,0:T(8,128)(2,1)S(1)} %bitcast.17), channel_id=1, replica_groups=mesh['dp'=64,'mp'=8] {'mp'}, dimensions={0} | all-to-all | bytes 1048576 | tf_op jit(solution)/shard_map/all_to_all | solution.py:180
  126.5 1.1 shard_map.107
  (11 shorter events, 0.1 us)
Async XLA Ops:
  0.6 1.0 copy-start
  1.7 0.7 copy-start.4
  3.4 11.1 %copy-start.5 = (s32[128,32]{0,1:T(8,128)S(1)}, s32[128,32]{0,1:T(8,128)}, u32[]{:S(2)}) copy-start(s32[128,32]{0,1:T(8,128)} %param.13) | copy-start | bytes 49156
  3.4 19.9 %all-to-all-start = ((bf16[8,256,128]{2,1,0:T(8,128)(2,1)}), bf16[8,256,128]{2,1,0:T(8,128)(2,1)S(1)}, u32[]{:S(2)}, u32[]{:S(2)}) async-start(bf16[8,256,128]{2,1,0:T(8,128)(2,1)} %shard_map.103), calls=%async_computation | async-start | bytes 1048576 | tf_op jit(solution)/shard_map/all_to_all | solution.py:139
  13.8 0.7 copy-start.6
  24.7 43.1 %copy-start.1 = (bf16[1,128,1024]{2,1,0:T(8,128)(2,1)S(1)}, bf16[1,128,1024]{2,1,0:T(8,128)(2,1)}, u32[]{:S(2)}) copy-start(bf16[1,128,1024]{2,1,0:T(8,128)(2,1)} %param.8) | copy-start | bytes 786436
  24.7 43.1 %copy-start.2 = (bf16[1,128,1024]{2,1,0:T(8,128)(2,1)S(1)}, bf16[1,128,1024]{2,1,0:T(8,128)(2,1)}, u32[]{:S(2)}) copy-start(bf16[1,128,1024]{2,1,0:T(8,128)(2,1)} %param.10) | copy-start | bytes 786436
  24.7 43.1 %copy-start.3 = (bf16[2,1,128,128]{3,2,1,0:T(8,128)(2,1)S(1)}, bf16[2,1,128,128]{3,2,1,0:T(8,128)(2,1)}, u32[]{:S(2)}) copy-start(bf16[2,1,128,128]{3,2,1,0:T(8,128)(2,1)} %param.9) | copy-start | bytes 196612
  24.7 43.1 %all-to-all-start.1 = ((bf16[64,32,128]{2,1,0:T(8,128)(2,1)}), bf16[64,32,128]{2,1,0:T(8,128)(2,1)S(1)}, u32[]{:S(2)}, u32[]{:S(2)}) async-start(bf16[64,32,128]{2,1,0:T(8,128)(2,1)} %shard_map.104), calls=%async_computation.1 | async-start | bytes 1048576 | tf_op jit(solution)/shard_map/all_to_all | solution.py:156
  72.4 38.0 %all-to-all-start.2 = ((bf16[64,32,128]{2,1,0:T(8,128)(2,1)}), bf16[64,32,128]{2,1,0:T(8,128)(2,1)S(1)}, u32[]{:S(2)}, u32[]{:S(2)}) async-start(bf16[64,32,128]{2,1,0:T(8,128)(2,1)} %get-tuple-element.8), calls=%async_computation.2 | async-start | bytes 1048576 | tf_op jit(solution)/shard_map/all_to_all | solution.py:171

commit v2 on v1

v2 whole, which is shorter than its diff:
```python
import functools
import math

import jax
import jax.numpy as jnp
from jax import lax
from jax.experimental import pallas as pl
from jax.experimental.pallas import tpu as pltpu
from jax.sharding import PartitionSpec as P

DH = 128
LEAD_DP = 42
SMEM = pl.BlockSpec(memory_space=pltpu.SMEM)
VMEM = pl.BlockSpec(memory_space=pltpu.VMEM)
HBM = pl.BlockSpec(memory_space=pltpu.MemorySpace.HBM)
PARAMS = pltpu.CompilerParams(vmem_limit_bytes=48 * 1024 * 1024)
INV_ROOT = 1.0 / DH**0.5
TO_EXP2 = math.log2(math.e) / DH**0.5
ACROSS = (((1,), (1,)), ((), ()))


def scale_kernel(chunks, pages_ref, scales_ref, out_ref, pages, scales, scaled, in_sems, out_sems, scales_sem):
    rows = pages_ref.shape[0]
    groups, heads = scales_ref.shape
    step = rows // chunks
    parts = [pl.ds(c * step, step) for c in range(chunks)]
    arriving = [
        pltpu.make_async_copy(pages_ref.at[part], pages.at[part], in_sems.at[c])
        for c, part in enumerate(parts)
    ]
    leaving = [
        pltpu.make_async_copy(scaled.at[:, part], out_ref.at[:, part], out_sems.at[c])
        for c, part in enumerate(parts)
    ]
    scales_copy = pltpu.make_async_copy(scales_ref, scales, scales_sem)
    scales_copy.start()
    for copy in arriving:
        copy.start()
    scales_copy.wait()
    factors = scales[...].astype(jnp.float32)
    factors = jnp.broadcast_to(factors[:, None, :], (groups, rows // groups, heads)).reshape(rows, heads)
    for c in range(chunks):
        arriving[c].wait()
        for j in range(heads):
            stored = pages[c * step : (c + 1) * step, j * DH : (j + 1) * DH].astype(jnp.float32)
            factor = factors[c * step : (c + 1) * step, j : j + 1]
            scaled[j, c * step : (c + 1) * step] = (stored * factor).astype(jnp.bfloat16)
        leaving[c].start()
    for copy in leaving:
        copy.wait()


def index_kernel(send_ref, sum_ref, source_ref, send_out, sum_out, source_out):
    for i in range(send_ref.shape[0]):
        send_out[i] = send_ref[i]
        sum_out[i] = sum_ref[i]
    for i in range(source_ref.shape[0]):
        source_out[i] = source_ref[i]


def select_kernel(rows_ref, pages_ref, out_ref):
    for r in range(out_ref.shape[0]):
        out_ref[r] = pages_ref[rows_ref[r]]


def own_kernel(length_ref, own_ref, q_ref, g_ref, q_rows_ref, g_rows_ref, top_ref, sum_ref, dot_ref):
    resp_len = q_ref.shape[0]
    live = lax.broadcasted_iota(jnp.int32, (resp_len, DH), 0) < length_ref[0]
    key_pos = lax.broadcasted_iota(jnp.int32, (resp_len, resp_len), 0)
    row_pos = lax.broadcasted_iota(jnp.int32, (resp_len, resp_len), 1)
    for h in range(q_ref.shape[1] // DH):
        rows = slice(h * resp_len, (h + 1) * resp_len)
        q = q_ref[:, h * DH : (h + 1) * DH]
        g = g_ref[:, h * DH : (h + 1) * DH]
        g = jnp.where(live, g, jnp.zeros_like(g))
        q_rows_ref[rows] = q
        g_rows_ref[rows] = g
        scores = lax.dot_general(own_ref[0], q, ACROSS, preferred_element_type=jnp.float32)
        grad_weights = lax.dot_general(own_ref[1], g, ACROSS, preferred_element_type=jnp.float32)
        scores = jnp.where(key_pos <= row_pos, scores, -1e30)
        top = jnp.max(scores, axis=0, keepdims=True)
        exps = jnp.exp2((scores - top) * TO_EXP2)
        top_ref[:, rows] = top
        sum_ref[:, rows] = jnp.sum(exps, axis=0, keepdims=True)
        dot_ref[:, rows] = jnp.sum(exps * grad_weights, axis=0, keepdims=True)


def gather_pages(sources_ref, arrived_ref, key_ref, value_ref):
    page_rows = arrived_ref.shape[1] // 2
    for i in range(sources_ref.shape[0]):
        slot = sources_ref[i]
        rows = slice(i * page_rows, (i + 1) * page_rows)
        key_ref[rows] = arrived_ref[slot, :page_rows]
        value_ref[rows] = arrived_ref[slot, page_rows:]


def page_grad_kernel(
    sources_ref, arrived_ref, q_ref, g_ref, top_ref, sum_ref, dot_ref, sent_ref, key_ref, value_ref
):
    gather_pages(sources_ref, arrived_ref, key_ref, value_ref)
    q = q_ref[...]
    g = g_ref[...]
    scores = lax.dot_general(key_ref[...], q, ACROSS, preferred_element_type=jnp.float32)
    grad_weights = lax.dot_general(value_ref[...], g, ACROSS, preferred_element_type=jnp.float32)
    own_top = top_ref[...]
    top = jnp.maximum(jnp.max(scores, axis=0, keepdims=True), own_top)
    exps = jnp.exp2((scores - top) * TO_EXP2)
    back = jnp.exp2((own_top - top) * TO_EXP2)
    scale = 1.0 / (jnp.sum(exps, axis=0, keepdims=True) + back * sum_ref[...])
    delta = (jnp.sum(exps * grad_weights, axis=0, keepdims=True) + back * dot_ref[...]) * scale
    weights = exps * scale
    grad_scores = (weights * (grad_weights - delta)).astype(jnp.bfloat16)
    value_grad = jnp.dot(weights.astype(jnp.bfloat16), g, preferred_element_type=jnp.float32)
    key_grad = jnp.dot(grad_scores, q, preferred_element_type=jnp.float32) * INV_ROOT
    value_grad = value_grad.astype(jnp.bfloat16)
    key_grad = key_grad.astype(jnp.bfloat16)
    page_rows = arrived_ref.shape[1] // 2
    for i in range(sources_ref.shape[0]):
        slot = sources_ref[i]
        rows = slice(i * page_rows, (i + 1) * page_rows)
        sent_ref[slot, :page_rows] = key_grad[rows]
        sent_ref[slot, page_rows:] = value_grad[rows]


def own_grad_kernel(
    sources_ref, arrived_ref, own_ref, q_ref, g_ref, d_query_ref, d_own_ref, key_ref, value_ref
):
    resp_len = d_query_ref.shape[0]
    prompt_len = key_ref.shape[0] - resp_len
    gather_pages(sources_ref, arrived_ref, key_ref, value_ref)
    key_ref[prompt_len:] = own_ref[0]
    value_ref[prompt_len:] = own_ref[1]
    keys = key_ref[...]
    values = value_ref[...]
    keys_t = keys.astype(jnp.float32).T.astype(jnp.bfloat16)
    width = 2 * resp_len
    own_pos = lax.broadcasted_iota(jnp.int32, (resp_len, width), 0)
    row_pos = lax.broadcasted_iota(jnp.int32, (resp_len, width), 1) % resp_len
    allowed = own_pos <= row_pos
    key_grad = None
    value_grad = None
    for b in range(q_ref.shape[0] // width):
        q = q_ref[b * width : (b + 1) * width]
        g = g_ref[b * width : (b + 1) * width]
        scores = lax.dot_general(keys, q, ACROSS, preferred_element_type=jnp.float32)
        grad_weights = lax.dot_general(values, g, ACROSS, preferred_element_type=jnp.float32)
        own_scores = jnp.where(allowed, scores[prompt_len:], -1e30)
        scores = jnp.concatenate([scores[:prompt_len], own_scores], axis=0)
        exps = jnp.exp2((scores - jnp.max(scores, axis=0, keepdims=True)) * TO_EXP2)
        scale = 1.0 / jnp.sum(exps, axis=0, keepdims=True)
        delta = jnp.sum(exps * grad_weights, axis=0, keepdims=True) * scale
        weights = exps * scale
        grad_scores = (weights * (grad_weights - delta)).astype(jnp.bfloat16)
        own_weights = weights[prompt_len:].astype(jnp.bfloat16)
        part = jnp.dot(own_weights, g, preferred_element_type=jnp.float32)
        value_grad = part if value_grad is None else value_grad + part
        part = jnp.dot(grad_scores[prompt_len:], q, preferred_element_type=jnp.float32)
        key_grad = part if key_grad is None else key_grad + part
        d_q = jnp.dot(keys_t, grad_scores, preferred_element_type=jnp.float32) * INV_ROOT
        for k in range(2):
            head = 2 * b + k
            block = d_q[:, k * resp_len : (k + 1) * resp_len].T
            d_query_ref[:, head * DH : (head + 1) * DH] = block.astype(jnp.bfloat16)
    d_own_ref[0] = (key_grad * INV_ROOT).astype(jnp.bfloat16)
    d_own_ref[1] = value_grad.astype(jnp.bfloat16)


def sum_kernel(rows_ref, arrived_ref, out_ref, total_ref):
    pages = out_ref.shape[0]
    total_ref[...] = jnp.zeros_like(total_ref)
    for r in range(arrived_ref.shape[0]):
        row = rows_ref[r]
        total_ref[row] = total_ref[row] + arrived_ref[r].astype(jnp.float32)
    out_ref[...] = total_ref[:pages].astype(jnp.bfloat16)


def layout_kernel(parts_ref, out_ref):
    for j in range(parts_ref.shape[0]):
        out_ref[:, j * DH : (j + 1) * DH] = parts_ref[j].astype(jnp.float32)


def per_device(resp_q, resp_kv, d_out, lengths, fork, page_table, pool_pages, pool_scales):
    dp_size = lax.axis_size("dp")
    mp_size = lax.axis_size("mp")
    my_dp = lax.axis_index("dp")
    pool_dev, _, page_rows, _ = pool_pages.shape
    heads_kv = pool_scales.shape[-1]
    pages_prompt = page_table.shape[1]
    resp_len = resp_q.shape[1]
    q_rows_all = resp_len * (resp_q.shape[2] // DH)
    prompt_len = pages_prompt * page_rows
    total = prompt_len + resp_len
    group_rows = mp_size * pool_dev
    slot_rows = 2 * page_rows
    stored_rows = pool_dev * slot_rows
    bf16 = jnp.bfloat16

    chunks = 4
    by_head = pl.pallas_call(
        functools.partial(scale_kernel, chunks),
        out_shape=jax.ShapeDtypeStruct((heads_kv, stored_rows, DH), bf16),
        in_specs=[HBM, HBM],
        out_specs=HBM,
        scratch_shapes=[
            pltpu.VMEM((stored_rows, heads_kv * DH), bf16),
            pltpu.VMEM((pool_dev * 2, heads_kv), bf16),
            pltpu.VMEM((heads_kv, stored_rows, DH), bf16),
            pltpu.SemaphoreType.DMA((chunks,)),
            pltpu.SemaphoreType.DMA((chunks,)),
            pltpu.SemaphoreType.DMA,
        ],
    )(pool_pages.reshape(stored_rows, -1), pool_scales.reshape(pool_dev * 2, heads_kv))
    regrouped = lax.all_to_all(by_head, "mp", split_axis=0, concat_axis=0, tiled=True)
    regrouped = regrouped.reshape(group_rows, slot_rows, DH)

    wanted = jnp.take(page_table, fork, axis=0)
    on_device = wanted // group_rows == my_dp
    send_rows = jnp.sum(jnp.where(on_device, wanted % group_rows, 0), axis=1)
    sum_rows = jnp.where(jnp.any(on_device, axis=1), send_rows, group_rows)
    sources = jnp.take(wanted, my_dp, axis=0) // group_rows
    lead = LEAD_DP % dp_size
    order = [[(lead + k) % dp_size for k in range(dp_size)]]
    send_rows = jnp.roll(send_rows, -lead)
    sum_rows = jnp.roll(sum_rows, -lead)
    sources = (sources - lead) % dp_size
    send_rows, sum_rows, sources = pl.pallas_call(
        index_kernel,
        out_shape=tuple(pltpu.MemorySpace.SMEM(v.shape, v.dtype) for v in (send_rows, sum_rows, sources)),
        in_specs=[SMEM, SMEM, SMEM],
        out_specs=(SMEM, SMEM, SMEM),
        compiler_params=PARAMS,
    )(send_rows, sum_rows, sources)

    own = resp_kv[:, 0]
    rows = jax.ShapeDtypeStruct((q_rows_all, DH), bf16)
    stat = jax.ShapeDtypeStruct((1, q_rows_all), jnp.float32)
    q_rows, g_rows, *stats = pl.pallas_call(
        own_kernel,
        out_shape=(rows, rows, stat, stat, stat),
        in_specs=[SMEM, VMEM, VMEM, VMEM],
        out_specs=(VMEM,) * 5,
        compiler_params=PARAMS,
        cost_estimate=pl.CostEstimate(flops=10**8, bytes_accessed=2**21, transcendentals=2**17),
    )(lengths, own, resp_q[0], d_out[0])
    send_rows, q_rows, g_rows = lax.optimization_barrier((send_rows, q_rows, g_rows))

    slots = jax.ShapeDtypeStruct((dp_size, slot_rows, DH), bf16)
    selected = pl.pallas_call(
        select_kernel,
        out_shape=slots,
        in_specs=[SMEM, VMEM],
        out_specs=VMEM,
        compiler_params=PARAMS,
    )(send_rows, regrouped)
    arrived = lax.all_to_all(selected, "dp", split_axis=0, concat_axis=0, axis_index_groups=order, tiled=True)

    sent = pl.pallas_call(
        page_grad_kernel,
        out_shape=slots,
        in_specs=[SMEM] + [VMEM] * 6,
        out_specs=VMEM,
        scratch_shapes=[pltpu.VMEM((prompt_len, DH), bf16), pltpu.VMEM((prompt_len, DH), bf16)],
        compiler_params=PARAMS,
    )(sources, arrived, q_rows, g_rows, *stats)
    returned = lax.all_to_all(sent, "dp", split_axis=0, concat_axis=0, axis_index_groups=order, tiled=True)

    d_query, d_own = pl.pallas_call(
        own_grad_kernel,
        out_shape=(
            jax.ShapeDtypeStruct(resp_q.shape[1:], bf16),
            jax.ShapeDtypeStruct((2, resp_len, DH), bf16),
        ),
        in_specs=[SMEM] + [VMEM] * 4,
        out_specs=(VMEM, VMEM),
        scratch_shapes=[pltpu.VMEM((total, DH), bf16), pltpu.VMEM((total, DH), bf16)],
        compiler_params=PARAMS,
        cost_estimate=pl.CostEstimate(flops=2 * 10**9, bytes_accessed=2**22, transcendentals=2**20),
    )(sources, arrived, own, q_rows, g_rows)

    summed = pl.pallas_call(
        sum_kernel,
        out_shape=jax.ShapeDtypeStruct((group_rows, slot_rows, DH), bf16),
        in_specs=[SMEM, VMEM],
        out_specs=VMEM,
        scratch_shapes=[pltpu.VMEM((group_rows + 1, slot_rows, DH), jnp.float32)],
        compiler_params=PARAMS,
    )(sum_rows, returned)
    restored = lax.all_to_all(
        summed.reshape(mp_size, stored_rows, DH), "mp", split_axis=0, concat_axis=0, tiled=True
    )
    d_pool = pl.pallas_call(
        layout_kernel,
        out_shape=jax.ShapeDtypeStruct((stored_rows, heads_kv * DH), jnp.float32),
        in_specs=[VMEM],
        out_specs=VMEM,
        compiler_params=PARAMS,
    )(restored)
    return d_query[None], d_own[:, None], d_pool.reshape(pool_pages.shape)


def solution(mesh):
    return jax.shard_map(
        per_device,
        mesh=mesh,
        in_specs=(
            P("dp", None, "mp"),
            P(None, "dp", None, "mp"),
            P("dp", None, "mp"),
            P("dp"),
            P(),
            P(),
            P(("dp", "mp"), None, None, None),
            P(("dp", "mp"), None, None),
        ),
        out_specs=(
            P("dp", None, "mp"),
            P(None, "dp", None, "mp"),
            P(("dp", "mp"), None, None, None),
        ),
        check_vma=False,
    )
```

time: 128 us -> 119 us (0.930)
  blocking collectives: 15.2 us -> 76.6 us
  waiting for transfers between devices: 65.2 us -> 11.8 us
  starting transfers between devices: 33.4 us -> 15.9 us
  Pallas kernels: 9 us -> 10.8 us
  local copies, waits for them, and re-layouts: 3.09 us -> 1.52 us
    all_to_all x1 -> x2, blocking collectives: 15.2 us -> 76.6 us  [the longest x1 40.5 us: per_device(): lax.all_to_all(selected, 'dp', split_axis=0, concat_axis=0, axis_index_gr...]
    all_to_all x2 -> x1, waiting for transfers between devices: 57.4 us -> 6.21 us  [per_device(): lax.all_to_all(summed.reshape(mp_size, stored_rows, DH), 'mp', split_axis...]
    all_to_all x2 -> x1, starting transfers between devices: 23 us -> 5.53 us  [per_device(): lax.all_to_all(summed.reshape(mp_size, stored_rows, DH), 'mp', split_axis...]
    pallas_call x3 -> x6, Pallas kernels: 6.68 us -> 9.55 us  [the longest x1 3.29 us: per_device(): pl.pallas_call(own_grad_kernel, out_shape=(jax.ShapeDtypeStruct(resp_q.sh...]
    all_to_all x1, waiting for transfers between devices: 7.8 us -> 5.59 us  [per_device(): lax.all_to_all(by_head, 'mp', split_axis=0, concat_axis=0, tiled=True)]
    unnamed x15 -> x11, local copies, waits for them, and re-layouts: 2.49 us -> 0.78 us
    pallas_call x1, Pallas kernels: 1.39 us -> 0.06 us  [per_device(): pl.pallas_call(select_kernel, out_shape=slots, in_specs=[SMEM, VMEM], out...]
  transfers between devices with their start and end apart: 3 -> 2, of which waited for: 3 -> 2; matrix products, arithmetic and copies ran while one was open for 1% -> 1% of each run, Pallas kernels for 0% -> 4%
where the time goes in v2:
time: 119 us
  blocking collectives  76.6 us (64%)
  starting transfers between devices  15.9 us (13%)
  waiting for transfers between devices  11.8 us (10%)
  Pallas kernels  10.8 us (9%)
  local copies, waits for them, and re-layouts  1.52 us (1%)
  between operations  1.41 us (1%)
    all_to_all x1, blocking collectives, per_device(): lax.all_to_all(selected, 'dp', split_axis=0, concat_axis=0, axis_index_gr...  40.5 us
    all_to_all x1, blocking collectives, per_device(): lax.all_to_all(sent, 'dp', split_axis=0, concat_axis=0, axis_index_groups...  36.1 us
    all_to_all x1, starting transfers between devices, per_device(): lax.all_to_all(by_head, 'mp', split_axis=0, concat_axis=0, tiled=True)  10.4 us
    all_to_all x1, waiting for transfers between devices, per_device(): lax.all_to_all(summed.reshape(mp_size, stored_rows, DH), 'mp', split_axis...  6.21 us
    all_to_all x1, waiting for transfers between devices, per_device(): lax.all_to_all(by_head, 'mp', split_axis=0, concat_axis=0, tiled=True)  5.59 us
    all_to_all x1, starting transfers between devices, per_device(): lax.all_to_all(summed.reshape(mp_size, stored_rows, DH), 'mp', split_axis...  5.53 us
    pallas_call x1, Pallas kernels, per_device(): pl.pallas_call(own_grad_kernel, out_shape=(jax.ShapeDtypeStruct(resp_q.sh...  3.29 us
  transfers between devices with their start and end apart: 2, of which 2 were waited for; matrix products, arithmetic and copies ran while one was open for 1% of the time, Pallas kernels for 4%

profile of v2, /device:TPU:1, one launch (start us, length us, event | category | flops | bytes accessed | tf_op | source)
XLA Modules:
  0.0 118.5 jit_solution(13729014068252444398)
XLA Ops:
  0.6 2.1 %shard_map.105 = bf16[8,256,128]{2,1,0:T(8,128)(2,1)} custom-call(bf16[256,1024]{1,0:T(8,128)(2,1)} %bitcast.26, bf16[16,8]{1,0:T(8,128)(2,1)} %bitcast.27), custom_call_target="tpu_custom_call" | custom-call | tf_op jit(solution)/shard_map/pallas_call | solution.py:199
  2.7 0.0 copy-start.3
  2.7 0.0 copy-start.2
  2.8 10.4 %all-to-all-start = ((bf16[8,256,128]{2,1,0:T(8,128)(2,1)}), bf16[8,256,128]{2,1,0:T(8,128)(2,1)S(1)}, u32[]{:S(2)}, u32[]{:S(2)}) async-start(bf16[8,256,128]{2,1,0:T(8,128)(2,1)} %shard_map.105), calls=%async_computation | async-start | bytes 1048576 | tf_op jit(solution)/shard_map/all_to_all | solution.py:213
  13.2 0.7 copy-done.4
  13.9 0.1 copy.11
  14.0 0.6 gather_fusion
  14.6 0.2 fusion.7
  14.8 0.1 fusion.2
  14.9 0.1 slice.14
  15.0 0.1 slice.16
  15.7 0.1 pad_add_fusion
  15.8 0.7 shard_map.103
  16.5 0.5 shard_map.104
  17.1 5.6 %all-to-all-done = bf16[8,256,128]{2,1,0:T(8,128)(2,1)S(1)} async-done(((bf16[8,256,128]{2,1,0:T(8,128)(2,1)}), bf16[8,256,128]{2,1,0:T(8,128)(2,1)S(1)}, u32[]{:S(2)}, u32[]{:S(2)}) %all-to-all-start) | async-done | bytes 524320 | tf_op jit(solution)/shard_map/all_to_all | solution.py:213
  22.7 0.1 shard_map.106
  22.7 40.5 %all_to_all.20.arrived_ref = bf16[64,32,128]{2,1,0:T(8,128)(2,1)S(1)} all-to-all(bf16[64,32,128]{2,1,0:T(8,128)(2,1)S(1)} %shard_map.106), channel_id=1, replica_groups={{336,344,352,360,368,376,384,392,400,408,416,424,432,440,448,456,464,47..., dimensions={0} | all-to-all | bytes 1048576 | tf_op jit(solution)/shard_map/all_to_all | solution.py:255
  63.2 1.9 %shard_map.108 = bf16[64,32,128]{2,1,0:T(8,128)(2,1)S(1)} custom-call(s32[32]{0:T(128)S(4)} %get-tuple-element.16.sources_ref, bf16[64,32,128]{2,1,0:T(8,128)(2,1)S(1)} %all_to_all.20.arrived_ref, bf16[1024,128]{1,0:T(8,128)(2,1)S(1)} %get-tuple-element.21.q_ref, bf16[1024,128]{1,0:T(8,128)(2,1)S(1)} %get-tuple-element.22.g_ref, ...), custom_call_target="tpu_custom_call" | custom-call | tf_op jit(solution)/shard_map/pallas_call | solution.py:257
  65.1 36.1 %all_to_all.21.arrived_ref = bf16[64,32,128]{2,1,0:T(8,128)(2,1)S(1)} all-to-all(bf16[64,32,128]{2,1,0:T(8,128)(2,1)S(1)} %shard_map.108), channel_id=1, replica_groups={{336,344,352,360,368,376,384,392,400,408,416,424,432,440,448,456,464,47..., dimensions={0} | all-to-all | bytes 1048576 | tf_op jit(solution)/shard_map/all_to_all | solution.py:265
  101.2 1.2 %shard_map.109 = bf16[64,32,128]{2,1,0:T(8,128)(2,1)} custom-call(s32[64]{0:T(128)S(4)} %get-tuple-element.25.rows_ref, bf16[64,32,128]{2,1,0:T(8,128)(2,1)S(1)} %all_to_all.21.arrived_ref), custom_call_target="tpu_custom_call" | custom-call | tf_op jit(solution)/shard_map/pallas_call | solution.py:280
  102.4 5.5 %all-to-all-start.3 = ((bf16[8,256,128]{2,1,0:T(8,128)(2,1)}), bf16[8,256,128]{2,1,0:T(8,128)(2,1)S(1)}, u32[]{:S(2)}, u32[]{:S(2)}) async-start(bf16[8,256,128]{2,1,0:T(8,128)(2,1)} %bitcast.10), calls=%async_computation.3 | async-start | bytes 1048576 | tf_op jit(solution)/shard_map/all_to_all | solution.py:288
  107.9 3.3 %shard_map.107 = (bf16[128,1024]{1,0:T(8,128)(2,1)}, bf16[2,128,128]{2,1,0:T(8,128)(2,1)}) custom-call(s32[32]{0:T(128)S(4)} %get-tuple-element.16.sources_ref, bf16[64,32,128]{2,1,0:T(8,128)(2,1)S(1)} %all_to_all.20.arrived_ref, bf16[2,128,128]{2,1,0:T(8,128)(2,1)S(1)} %bitcast.24, bf16[1024,128]{1,0:T(8,128)(2,1)S(1)} %get-tuple-element.21.q_ref, ...), custom_call_target="tpu_custom_call" | custom-call | flops 2000000000 | bytes 4194304 | tf_op jit(solution)/shard_map/pallas_call | solution.py:267
  111.2 6.2 %all-to-all-done.3.parts_ref = bf16[8,256,128]{2,1,0:T(8,128)(2,1)S(1)} async-done(((bf16[8,256,128]{2,1,0:T(8,128)(2,1)}), bf16[8,256,128]{2,1,0:T(8,128)(2,1)S(1)}, u32[]{:S(2)}, u32[]{:S(2)}) %all-to-all-start.3) | async-done | bytes 524320 | tf_op jit(solution)/shard_map/all_to_all | solution.py:288
  117.4 1.1 shard_map.110
  (12 shorter events, 0.1 us)
Async XLA Ops:
  2.7 11.1 %copy-start.3 = (s32[128,32]{0,1:T(8,128)S(1)}, s32[128,32]{0,1:T(8,128)}, u32[]{:S(2)}) copy-start(s32[128,32]{0,1:T(8,128)} %param.13) | copy-start | bytes 49156
  2.7 13.8 %copy-start.2 = (bf16[2,1,128,128]{3,2,1,0:T(8,128)(2,1)S(1)}, bf16[2,1,128,128]{3,2,1,0:T(8,128)(2,1)}, u32[]{:S(2)}) copy-start(bf16[2,1,128,128]{3,2,1,0:T(8,128)(2,1)} %param.9) | copy-start | bytes 196612
  2.8 19.9 %all-to-all-start = ((bf16[8,256,128]{2,1,0:T(8,128)(2,1)}), bf16[8,256,128]{2,1,0:T(8,128)(2,1)S(1)}, u32[]{:S(2)}, u32[]{:S(2)}) async-start(bf16[8,256,128]{2,1,0:T(8,128)(2,1)} %shard_map.105), calls=%async_computation | async-start | bytes 1048576 | tf_op jit(solution)/shard_map/all_to_all | solution.py:213
  13.2 0.7 copy-start.4
  13.9 2.7 %copy-start = (bf16[1,128,1024]{2,1,0:T(8,128)(2,1)S(1)}, bf16[1,128,1024]{2,1,0:T(8,128)(2,1)}, u32[]{:S(2)}) copy-start(bf16[1,128,1024]{2,1,0:T(8,128)(2,1)} %param.8) | copy-start | bytes 786436
  13.9 2.7 %copy-start.1 = (bf16[1,128,1024]{2,1,0:T(8,128)(2,1)S(1)}, bf16[1,128,1024]{2,1,0:T(8,128)(2,1)}, u32[]{:S(2)}) copy-start(bf16[1,128,1024]{2,1,0:T(8,128)(2,1)} %param.10) | copy-start | bytes 786436
  102.4 15.0 %all-to-all-start.3 = ((bf16[8,256,128]{2,1,0:T(8,128)(2,1)}), bf16[8,256,128]{2,1,0:T(8,128)(2,1)S(1)}, u32[]{:S(2)}, u32[]{:S(2)}) async-start(bf16[8,256,128]{2,1,0:T(8,128)(2,1)} %bitcast.10), calls=%async_computation.3 | async-start | bytes 1048576 | tf_op jit(solution)/shard_map/all_to_all | solution.py:288

commit v3 on v2

--- a/solution.py
+++ b/solution.py
@@ -9,7 +9,8 @@
 from jax.sharding import PartitionSpec as P
 
 DH = 128
-LEAD_DP = 42
+LEAD_DP = 26
+LEAD_MP = 4
 SMEM = pl.BlockSpec(memory_space=pltpu.SMEM)
 VMEM = pl.BlockSpec(memory_space=pltpu.VMEM)
 HBM = pl.BlockSpec(memory_space=pltpu.MemorySpace.HBM)
@@ -19,7 +20,9 @@
 ACROSS = (((1,), (1,)), ((), ()))
 
 
-def scale_kernel(chunks, pages_ref, scales_ref, out_ref, pages, scales, scaled, in_sems, out_sems, scales_sem):
+def scale_kernel(
+    chunks, order, pages_ref, scales_ref, out_ref, pages, scales, scaled, in_sems, out_sems, scales_sem
+):
     rows = pages_ref.shape[0]
     groups, heads = scales_ref.shape
     step = rows // chunks
@@ -41,21 +44,31 @@
     factors = jnp.broadcast_to(factors[:, None, :], (groups, rows // groups, heads)).reshape(rows, heads)
     for c in range(chunks):
         arriving[c].wait()
-        for j in range(heads):
+        for k, j in enumerate(order):
             stored = pages[c * step : (c + 1) * step, j * DH : (j + 1) * DH].astype(jnp.float32)
             factor = factors[c * step : (c + 1) * step, j : j + 1]
-            scaled[j, c * step : (c + 1) * step] = (stored * factor).astype(jnp.bfloat16)
+            scaled[k, c * step : (c + 1) * step] = (stored * factor).astype(jnp.bfloat16)
         leaving[c].start()
     for copy in leaving:
         copy.wait()
 
 
-def index_kernel(send_ref, sum_ref, source_ref, send_out, sum_out, source_out):
-    for i in range(send_ref.shape[0]):
-        send_out[i] = send_ref[i]
-        sum_out[i] = sum_ref[i]
+def dp_order(size):
+    return [(LEAD_DP + k) % size for k in range(size)]
+
+
+def mp_order(size):
+    return [(LEAD_MP + k) % size for k in range(size)]
+
+
+def index_kernel(order, shift, send_ref, found_ref, source_ref, place_ref, send_out, sum_out, source_out):
+    pages = len(order)
+    for k, r in enumerate(order):
+        row = lax.rem(send_ref[r] + shift, pages)
+        send_out[k] = row
+        sum_out[k] = jnp.where(found_ref[r] > 0, row, pages)
     for i in range(source_ref.shape[0]):
-        source_out[i] = source_ref[i]
+        source_out[i] = place_ref[source_ref[i]]
 
 
 def select_kernel(rows_ref, pages_ref, out_ref):
@@ -174,9 +187,15 @@
     out_ref[...] = total_ref[:pages].astype(jnp.bfloat16)
 
 
-def layout_kernel(parts_ref, out_ref):
-    for j in range(parts_ref.shape[0]):
-        out_ref[:, j * DH : (j + 1) * DH] = parts_ref[j].astype(jnp.float32)
+def layout_kernel(order, parts_ref, out_ref):
+    for k, j in enumerate(order):
+        out_ref[:, j * DH : (j + 1) * DH] = parts_ref[k].astype(jnp.float32)
+
+
+def exchange(parts, axis, order):
+    return lax.all_to_all(
+        parts, axis, split_axis=0, concat_axis=0, axis_index_groups=[order], tiled=True
+    )
 
 
 def per_device(resp_q, resp_kv, d_out, lengths, fork, page_table, pool_pages, pool_scales):
@@ -195,9 +214,12 @@
     stored_rows = pool_dev * slot_rows
     bf16 = jnp.bfloat16
 
+    order = dp_order(dp_size)
+    heads = mp_order(mp_size)
+
     chunks = 4
     by_head = pl.pallas_call(
-        functools.partial(scale_kernel, chunks),
+        functools.partial(scale_kernel, chunks, heads),
         out_shape=jax.ShapeDtypeStruct((heads_kv, stored_rows, DH), bf16),
         in_specs=[HBM, HBM],
         out_specs=HBM,
@@ -210,26 +232,22 @@
             pltpu.SemaphoreType.DMA,
         ],
     )(pool_pages.reshape(stored_rows, -1), pool_scales.reshape(pool_dev * 2, heads_kv))
-    regrouped = lax.all_to_all(by_head, "mp", split_axis=0, concat_axis=0, tiled=True)
+    regrouped = exchange(by_head, "mp", heads)
     regrouped = regrouped.reshape(group_rows, slot_rows, DH)
 
     wanted = jnp.take(page_table, fork, axis=0)
     on_device = wanted // group_rows == my_dp
     send_rows = jnp.sum(jnp.where(on_device, wanted % group_rows, 0), axis=1)
-    sum_rows = jnp.where(jnp.any(on_device, axis=1), send_rows, group_rows)
+    found = jnp.sum(on_device.astype(jnp.int32), axis=1)
     sources = jnp.take(wanted, my_dp, axis=0) // group_rows
-    lead = LEAD_DP % dp_size
-    order = [[(lead + k) % dp_size for k in range(dp_size)]]
-    send_rows = jnp.roll(send_rows, -lead)
-    sum_rows = jnp.roll(sum_rows, -lead)
-    sources = (sources - lead) % dp_size
+    place = jnp.asarray([order.index(d) for d in range(dp_size)], jnp.int32)
     send_rows, sum_rows, sources = pl.pallas_call(
-        index_kernel,
-        out_shape=tuple(pltpu.MemorySpace.SMEM(v.shape, v.dtype) for v in (send_rows, sum_rows, sources)),
-        in_specs=[SMEM, SMEM, SMEM],
+        functools.partial(index_kernel, order, group_rows - heads[0] * pool_dev),
+        out_shape=tuple(pltpu.MemorySpace.SMEM(v.shape, v.dtype) for v in (send_rows, found, sources)),
+        in_specs=[SMEM, SMEM, SMEM, SMEM],
         out_specs=(SMEM, SMEM, SMEM),
         compiler_params=PARAMS,
-    )(send_rows, sum_rows, sources)
+    )(send_rows, found, sources, place)
 
     own = resp_kv[:, 0]
     rows = jax.ShapeDtypeStruct((q_rows_all, DH), bf16)
@@ -252,7 +270,7 @@
         out_specs=VMEM,
         compiler_params=PARAMS,
     )(send_rows, regrouped)
-    arrived = lax.all_to_all(selected, "dp", split_axis=0, concat_axis=0, axis_index_groups=order, tiled=True)
+    arrived = exchange(selected, "dp", order)
 
     sent = pl.pallas_call(
         page_grad_kernel,
@@ -262,7 +280,7 @@
         scratch_shapes=[pltpu.VMEM((prompt_len, DH), bf16), pltpu.VMEM((prompt_len, DH), bf16)],
         compiler_params=PARAMS,
     )(sources, arrived, q_rows, g_rows, *stats)
-    returned = lax.all_to_all(sent, "dp", split_axis=0, concat_axis=0, axis_index_groups=order, tiled=True)
+    returned = exchange(sent, "dp", order)
 
     d_query, d_own = pl.pallas_call(
         own_grad_kernel,
@@ -285,11 +303,9 @@
         scratch_shapes=[pltpu.VMEM((group_rows + 1, slot_rows, DH), jnp.float32)],
         compiler_params=PARAMS,
     )(sum_rows, returned)
-    restored = lax.all_to_all(
-        summed.reshape(mp_size, stored_rows, DH), "mp", split_axis=0, concat_axis=0, tiled=True
-    )
+    restored = exchange(summed.reshape(mp_size, stored_rows, DH), "mp", heads)
     d_pool = pl.pallas_call(
-        layout_kernel,
+        functools.partial(layout_kernel, heads),
         out_shape=jax.ShapeDtypeStruct((stored_rows, heads_kv * DH), jnp.float32),
         in_specs=[VMEM],
         out_specs=VMEM,

time: 119 us -> 118 us (level)
  waiting for transfers between devices: 11.8 us -> 6.74 us
  starting transfers between devices: 15.9 us -> 18.3 us
  blocking collectives: 76.6 us -> 78.2 us
    all_to_all x2, waiting for transfers between devices: 11.8 us -> 6.74 us  [exchange(): lax.all_to_all(parts, axis, split_axis=0, concat_axis=0, axis_index_group...]
    all_to_all x2, starting transfers between devices: 15.9 us -> 18.3 us  [exchange(): lax.all_to_all(parts, axis, split_axis=0, concat_axis=0, axis_index_group...]
    all_to_all x2, blocking collectives: 76.6 us -> 78.2 us  [exchange(): lax.all_to_all(parts, axis, split_axis=0, concat_axis=0, axis_index_group...]
where the time goes in v3:
time: 118 us; the launch traced here: 117 us
  blocking collectives  78.2 us (66%)
  starting transfers between devices  18.3 us (16%)
  Pallas kernels  11 us (9%)
  waiting for transfers between devices  6.74 us (6%)
  between operations  1.46 us (1%)
  local copies, waits for them, and re-layouts  1.38 us (1%)
    all_to_all x2, blocking collectives, exchange(): lax.all_to_all(parts, axis, split_axis=0, concat_axis=0, axis_index_group...  78.2 us
    all_to_all x2, starting transfers between devices, exchange(): lax.all_to_all(parts, axis, split_axis=0, concat_axis=0, axis_index_group...  18.3 us
    all_to_all x2, waiting for transfers between devices, exchange(): lax.all_to_all(parts, axis, split_axis=0, concat_axis=0, axis_index_group...  6.74 us
    pallas_call x1, Pallas kernels, per_device(): pl.pallas_call(own_grad_kernel, out_shape=(jax.ShapeDtypeStruct(resp_q.sh...  3.31 us
  transfers between devices with their start and end apart: 2, of which 2 were waited for; matrix products, arithmetic and copies ran while one was open for 1% of the time, Pallas kernels for 4%

profile of v3, /device:TPU:1, one launch (start us, length us, event | category | flops | bytes accessed | tf_op | source)
XLA Modules:
  0.0 117.3 jit_solution(12612459061133718746)
XLA Ops:
  0.6 2.1 %shard_map.114 = bf16[8,256,128]{2,1,0:T(8,128)(2,1)} custom-call(bf16[256,1024]{1,0:T(8,128)(2,1)} %bitcast.22, bf16[16,8]{1,0:T(8,128)(2,1)} %bitcast.23), custom_call_target="tpu_custom_call" | custom-call | tf_op jit(solution)/shard_map/pallas_call | solution.py:221
  2.7 0.0 copy-start.4
  2.7 0.0 copy-start.3
  2.8 0.0 copy-start.2
  2.8 11.5 %all-to-all-start = ((bf16[8,256,128]{2,1,0:T(8,128)(2,1)}), bf16[8,256,128]{2,1,0:T(8,128)(2,1)S(1)}, u32[]{:S(2)}, u32[]{:S(2)}) async-start(bf16[8,256,128]{2,1,0:T(8,128)(2,1)} %shard_map.114), calls=%async_computation | async-start | bytes 1048576 | tf_op jit(solution)/shard_map/all_to_all | solution.py:196
  14.2 0.7 copy-done.5
  14.9 0.0 copy-start
  14.9 0.0 copy-start.1
  14.9 0.1 copy.12
  15.7 0.6 gather_fusion
  16.3 0.1 fusion
  16.5 0.1 convert_reduce_fusion
  16.6 0.9 shard_map.112
  17.5 0.5 shard_map.113
  18.0 3.2 %all-to-all-done = bf16[8,256,128]{2,1,0:T(8,128)(2,1)S(1)} async-done(((bf16[8,256,128]{2,1,0:T(8,128)(2,1)}), bf16[8,256,128]{2,1,0:T(8,128)(2,1)S(1)}, u32[]{:S(2)}, u32[]{:S(2)}) %all-to-all-start) | async-done | bytes 524320 | tf_op jit(solution)/shard_map/all_to_all | solution.py:196
  21.2 0.1 shard_map.115
  21.3 40.7 %all_to_all.20.arrived_ref = bf16[64,32,128]{2,1,0:T(8,128)(2,1)S(1)} all-to-all(bf16[64,32,128]{2,1,0:T(8,128)(2,1)S(1)} %shard_map.115), channel_id=1, replica_groups={{208,216,224,232,240,248,256,264,272,280,288,296,304,312,320,328,336,34..., dimensions={0} | all-to-all | bytes 1048576 | tf_op jit(solution)/shard_map/all_to_all | solution.py:196
  61.9 1.9 %shard_map.117 = bf16[64,32,128]{2,1,0:T(8,128)(2,1)S(1)} custom-call(s32[32]{0:T(128)S(4)} %get-tuple-element.16.sources_ref, bf16[64,32,128]{2,1,0:T(8,128)(2,1)S(1)} %all_to_all.20.arrived_ref, bf16[1024,128]{1,0:T(8,128)(2,1)S(1)} %get-tuple-element.21.q_ref, bf16[1024,128]{1,0:T(8,128)(2,1)S(1)} %get-tuple-element.22.g_ref, ...), custom_call_target="tpu_custom_call" | custom-call | tf_op jit(solution)/shard_map/pallas_call | solution.py:275
  63.8 37.5 %all_to_all.21.arrived_ref = bf16[64,32,128]{2,1,0:T(8,128)(2,1)S(1)} all-to-all(bf16[64,32,128]{2,1,0:T(8,128)(2,1)S(1)} %shard_map.117), channel_id=1, replica_groups={{208,216,224,232,240,248,256,264,272,280,288,296,304,312,320,328,336,34..., dimensions={0} | all-to-all | bytes 1048576 | tf_op jit(solution)/shard_map/all_to_all | solution.py:196
  101.3 1.2 shard_map.118
  102.5 6.8 %all-to-all-start.3 = ((bf16[8,256,128]{2,1,0:T(8,128)(2,1)}), bf16[8,256,128]{2,1,0:T(8,128)(2,1)S(1)}, u32[]{:S(2)}, u32[]{:S(2)}) async-start(bf16[8,256,128]{2,1,0:T(8,128)(2,1)} %bitcast.10), calls=%async_computation.3 | async-start | bytes 1048576 | tf_op jit(solution)/shard_map/all_to_all | solution.py:196
  109.3 3.3 %shard_map.116 = (bf16[128,1024]{1,0:T(8,128)(2,1)}, bf16[2,128,128]{2,1,0:T(8,128)(2,1)}) custom-call(s32[32]{0:T(128)S(4)} %get-tuple-element.16.sources_ref, bf16[64,32,128]{2,1,0:T(8,128)(2,1)S(1)} %all_to_all.20.arrived_ref, bf16[2,128,128]{2,1,0:T(8,128)(2,1)S(1)} %bitcast.20, bf16[1024,128]{1,0:T(8,128)(2,1)S(1)} %get-tuple-element.21.q_ref, ...), custom_call_target="tpu_custom_call" | custom-call | flops 2000000000 | bytes 4194304 | tf_op jit(solution)/shard_map/pallas_call | solution.py:285
  112.6 3.6 %all-to-all-done.3.parts_ref = bf16[8,256,128]{2,1,0:T(8,128)(2,1)S(1)} async-done(((bf16[8,256,128]{2,1,0:T(8,128)(2,1)}), bf16[8,256,128]{2,1,0:T(8,128)(2,1)S(1)}, u32[]{:S(2)}, u32[]{:S(2)}) %all-to-all-start.3) | async-done | bytes 524320 | tf_op jit(solution)/shard_map/all_to_all | solution.py:196
  116.2 1.1 shard_map.119
  (10 shorter events, 0.0 us)
Async XLA Ops:
  2.7 12.2 %copy-start.4 = (s32[128,32]{0,1:T(8,128)S(1)}, s32[128,32]{0,1:T(8,128)}, u32[]{:S(2)}) copy-start(s32[128,32]{0,1:T(8,128)} %param.14) | copy-start | bytes 49156
  2.7 13.8 %copy-start.3 = (s32[64]{0:T(128)S(1)}, s32[64]{0:T(128)}, u32[]{:S(2)}) copy-start(s32[64]{0:T(128)} %constant.75.clone.place_ref) | copy-start | bytes 772
  2.8 14.7 %copy-start.2 = (bf16[2,1,128,128]{3,2,1,0:T(8,128)(2,1)S(1)}, bf16[2,1,128,128]{3,2,1,0:T(8,128)(2,1)}, u32[]{:S(2)}) copy-start(bf16[2,1,128,128]{3,2,1,0:T(8,128)(2,1)} %param.10) | copy-start | bytes 196612
  2.8 18.4 %all-to-all-start = ((bf16[8,256,128]{2,1,0:T(8,128)(2,1)}), bf16[8,256,128]{2,1,0:T(8,128)(2,1)S(1)}, u32[]{:S(2)}, u32[]{:S(2)}) async-start(bf16[8,256,128]{2,1,0:T(8,128)(2,1)} %shard_map.114), calls=%async_computation | async-start | bytes 1048576 | tf_op jit(solution)/shard_map/all_to_all | solution.py:196
  14.2 0.7 copy-start.5
  14.9 2.6 %copy-start = (bf16[1,128,1024]{2,1,0:T(8,128)(2,1)S(1)}, bf16[1,128,1024]{2,1,0:T(8,128)(2,1)}, u32[]{:S(2)}) copy-start(bf16[1,128,1024]{2,1,0:T(8,128)(2,1)} %param.9) | copy-start | bytes 786436
  14.9 2.6 %copy-start.1 = (bf16[1,128,1024]{2,1,0:T(8,128)(2,1)S(1)}, bf16[1,128,1024]{2,1,0:T(8,128)(2,1)}, u32[]{:S(2)}) copy-start(bf16[1,128,1024]{2,1,0:T(8,128)(2,1)} %param.11) | copy-start | bytes 786436
  102.5 13.7 %all-to-all-start.3 = ((bf16[8,256,128]{2,1,0:T(8,128)(2,1)}), bf16[8,256,128]{2,1,0:T(8,128)(2,1)S(1)}, u32[]{:S(2)}, u32[]{:S(2)}) async-start(bf16[8,256,128]{2,1,0:T(8,128)(2,1)} %bitcast.10), calls=%async_computation.3 | async-start | bytes 1048576 | tf_op jit(solution)/shard_map/all_to_all | solution.py:196

commit v4 on v3

--- a/solution.py
+++ b/solution.py
@@ -9,7 +9,7 @@
 from jax.sharding import PartitionSpec as P
 
 DH = 128
-LEAD_DP = 26
+LEAD_DP = 27
 LEAD_MP = 4
 SMEM = pl.BlockSpec(memory_space=pltpu.SMEM)
 VMEM = pl.BlockSpec(memory_space=pltpu.VMEM)
@@ -21,8 +21,9 @@
 
 
 def scale_kernel(
-    chunks, order, pages_ref, scales_ref, out_ref, pages, scales, scaled, in_sems, out_sems, scales_sem
+    chunks, lists, pages_ref, scales_ref, *refs
 ):
+    (out0_ref, out1_ref, pages, scales, scaled0, scaled1, in_sems, out_sems, scales_sem) = refs
     rows = pages_ref.shape[0]
     groups, heads = scales_ref.shape
     step = rows // chunks
@@ -31,8 +32,10 @@
         pltpu.make_async_copy(pages_ref.at[part], pages.at[part], in_sems.at[c])
         for c, part in enumerate(parts)
     ]
+    outs = [(scaled0, out0_ref), (scaled1, out1_ref)]
     leaving = [
-        pltpu.make_async_copy(scaled.at[:, part], out_ref.at[:, part], out_sems.at[c])
+        pltpu.make_async_copy(scaled.at[:, part], out_ref.at[:, part], out_sems.at[core, c])
+        for core, (scaled, out_ref) in enumerate(outs)
         for c, part in enumerate(parts)
     ]
     scales_copy = pltpu.make_async_copy(scales_ref, scales, scales_sem)
@@ -44,11 +47,12 @@
     factors = jnp.broadcast_to(factors[:, None, :], (groups, rows // groups, heads)).reshape(rows, heads)
     for c in range(chunks):
         arriving[c].wait()
-        for k, j in enumerate(order):
-            stored = pages[c * step : (c + 1) * step, j * DH : (j + 1) * DH].astype(jnp.float32)
-            factor = factors[c * step : (c + 1) * step, j : j + 1]
-            scaled[k, c * step : (c + 1) * step] = (stored * factor).astype(jnp.bfloat16)
-        leaving[c].start()
+        for core, (scaled, _) in enumerate(outs):
+            for k, j in enumerate(lists[core]):
+                stored = pages[c * step : (c + 1) * step, j * DH : (j + 1) * DH].astype(jnp.float32)
+                factor = factors[c * step : (c + 1) * step, j : j + 1]
+                scaled[k, c * step : (c + 1) * step] = (stored * factor).astype(jnp.bfloat16)
+            leaving[core * chunks + c].start()
     for copy in leaving:
         copy.wait()
 
@@ -61,22 +65,47 @@
     return [(LEAD_MP + k) % size for k in range(size)]
 
 
-def index_kernel(order, shift, send_ref, found_ref, source_ref, place_ref, send_out, sum_out, source_out):
-    pages = len(order)
+def index_kernel(order, send_ref, sum_ref, source_ref, send_out, sum_out, source_out):
     for k, r in enumerate(order):
-        row = lax.rem(send_ref[r] + shift, pages)
-        send_out[k] = row
-        sum_out[k] = jnp.where(found_ref[r] > 0, row, pages)
+        send_out[k] = send_ref[r]
+        sum_out[k] = sum_ref[r]
     for i in range(source_ref.shape[0]):
-        source_out[i] = place_ref[source_ref[i]]
-
-
-def select_kernel(rows_ref, pages_ref, out_ref):
+        source_out[i] = source_ref[i]
+
+
+def select_kernel(rows_ref, first_ref, second_ref, out_ref):
+    half = first_ref.shape[0]
     for r in range(out_ref.shape[0]):
-        out_ref[r] = pages_ref[rows_ref[r]]
-
-
-def own_kernel(length_ref, own_ref, q_ref, g_ref, q_rows_ref, g_rows_ref, top_ref, sum_ref, dot_ref):
+        row = rows_ref[r]
+        place = lax.rem(row, half)
+        out_ref[r] = jnp.where(row < half, first_ref[place], second_ref[place])
+
+
+def select_chips_kernel(pages_dev, chip_ref, rows_ref, *refs):
+    *arrived_refs, out_ref, pages_ref = refs
+    chips = len(arrived_refs)
+    for d in range(chips):
+        pages_ref[d] = arrived_refs[d][...]
+    half = chips * pages_dev
+    for r in range(out_ref.shape[0]):
+        row = rows_ref[r]
+        core = lax.div(row, half)
+        place = lax.rem(row, half)
+        back = lax.rem(chip_ref[0] + chips - lax.div(place, pages_dev), chips)
+        out_ref[r] = pages_ref[back, core * pages_dev + lax.rem(place, pages_dev)]
+
+
+def pair_kernel(chip_ref, first_ref, second_ref, *out_refs):
+    chips = len(out_refs)
+    for d in range(chips):
+        chip = lax.rem(chip_ref[0] + d, chips)
+        out_refs[d][0] = first_ref[chip]
+        out_refs[d][1] = second_ref[chip]
+
+
+def own_kernel(
+    length_ref, own_ref, q_ref, g_ref, q_rows_ref, g_rows_ref, top_ref, sum_ref, exps_ref, grad_ref
+):
     resp_len = q_ref.shape[0]
     live = lax.broadcasted_iota(jnp.int32, (resp_len, DH), 0) < length_ref[0]
     key_pos = lax.broadcasted_iota(jnp.int32, (resp_len, resp_len), 0)
@@ -95,7 +124,8 @@
         exps = jnp.exp2((scores - top) * TO_EXP2)
         top_ref[:, rows] = top
         sum_ref[:, rows] = jnp.sum(exps, axis=0, keepdims=True)
-        dot_ref[:, rows] = jnp.sum(exps * grad_weights, axis=0, keepdims=True)
+        exps_ref[:, rows] = exps
+        grad_ref[:, rows] = grad_weights
 
 
 def gather_pages(sources_ref, arrived_ref, key_ref, value_ref):
@@ -108,7 +138,17 @@
 
 
 def page_grad_kernel(
-    sources_ref, arrived_ref, q_ref, g_ref, top_ref, sum_ref, dot_ref, sent_ref, key_ref, value_ref
+    sources_ref,
+    arrived_ref,
+    q_ref,
+    g_ref,
+    top_ref,
+    sum_ref,
+    own_exps_ref,
+    own_grad_ref,
+    sent_ref,
+    key_ref,
+    value_ref,
 ):
     gather_pages(sources_ref, arrived_ref, key_ref, value_ref)
     q = q_ref[...]
@@ -120,10 +160,13 @@
     exps = jnp.exp2((scores - top) * TO_EXP2)
     back = jnp.exp2((own_top - top) * TO_EXP2)
     scale = 1.0 / (jnp.sum(exps, axis=0, keepdims=True) + back * sum_ref[...])
-    delta = (jnp.sum(exps * grad_weights, axis=0, keepdims=True) + back * dot_ref[...]) * scale
     weights = exps * scale
+    weights_b = weights.astype(jnp.bfloat16)
+    own_weights = (own_exps_ref[...] * (back * scale)).astype(jnp.bfloat16)
+    delta = jnp.sum(weights_b.astype(jnp.float32) * grad_weights, axis=0, keepdims=True)
+    delta += jnp.sum(own_weights.astype(jnp.float32) * own_grad_ref[...], axis=0, keepdims=True)
     grad_scores = (weights * (grad_weights - delta)).astype(jnp.bfloat16)
-    value_grad = jnp.dot(weights.astype(jnp.bfloat16), g, preferred_element_type=jnp.float32)
+    value_grad = jnp.dot(weights_b, g, preferred_element_type=jnp.float32)
     key_grad = jnp.dot(grad_scores, q, preferred_element_type=jnp.float32) * INV_ROOT
     value_grad = value_grad.astype(jnp.bfloat16)
     key_grad = key_grad.astype(jnp.bfloat16)
@@ -161,11 +204,11 @@
         scores = jnp.concatenate([scores[:prompt_len], own_scores], axis=0)
         exps = jnp.exp2((scores - jnp.max(scores, axis=0, keepdims=True)) * TO_EXP2)
         scale = 1.0 / jnp.sum(exps, axis=0, keepdims=True)
-        delta = jnp.sum(exps * grad_weights, axis=0, keepdims=True) * scale
         weights = exps * scale
+        weights_b = weights.astype(jnp.bfloat16)
+        delta = jnp.sum(weights_b.astype(jnp.float32) * grad_weights, axis=0, keepdims=True)
         grad_scores = (weights * (grad_weights - delta)).astype(jnp.bfloat16)
-        own_weights = weights[prompt_len:].astype(jnp.bfloat16)
-        part = jnp.dot(own_weights, g, preferred_element_type=jnp.float32)
+        part = jnp.dot(weights_b[prompt_len:], g, preferred_element_type=jnp.float32)
         value_grad = part if value_grad is None else value_grad + part
         part = jnp.dot(grad_scores[prompt_len:], q, preferred_element_type=jnp.float32)
         key_grad = part if key_grad is None else key_grad + part
@@ -192,9 +235,9 @@
         out_ref[:, j * DH : (j + 1) * DH] = parts_ref[k].astype(jnp.float32)
 
 
-def exchange(parts, axis, order):
+def exchange(parts, axis, *groups):
     return lax.all_to_all(
-        parts, axis, split_axis=0, concat_axis=0, axis_index_groups=[order], tiled=True
+        parts, axis, split_axis=0, concat_axis=0, axis_index_groups=list(groups), tiled=True
     )
 
 
@@ -218,64 +261,115 @@
     heads = mp_order(mp_size)
 
     chunks = 4
-    by_head = pl.pallas_call(
-        functools.partial(scale_kernel, chunks, heads),
-        out_shape=jax.ShapeDtypeStruct((heads_kv, stored_rows, DH), bf16),
+    chips = mp_size // 2
+    first_y = heads[0] // 2
+    chip_order = [(first_y + k) % chips for k in range(chips)]
+    lists = [[2 * y + core for y in chip_order] for core in range(2)]
+    head_parts = jax.ShapeDtypeStruct((chips, stored_rows, DH), bf16)
+    of_core0, of_core1 = pl.pallas_call(
+        functools.partial(scale_kernel, chunks, lists),
+        out_shape=(head_parts, head_parts),
         in_specs=[HBM, HBM],
-        out_specs=HBM,
+        out_specs=(HBM, HBM),
         scratch_shapes=[
             pltpu.VMEM((stored_rows, heads_kv * DH), bf16),
             pltpu.VMEM((pool_dev * 2, heads_kv), bf16),
-            pltpu.VMEM((heads_kv, stored_rows, DH), bf16),
+            pltpu.VMEM((chips, stored_rows, DH), bf16),
+            pltpu.VMEM((chips, stored_rows, DH), bf16),
             pltpu.SemaphoreType.DMA((chunks,)),
-            pltpu.SemaphoreType.DMA((chunks,)),
+            pltpu.SemaphoreType.DMA((2, chunks)),
             pltpu.SemaphoreType.DMA,
         ],
     )(pool_pages.reshape(stored_rows, -1), pool_scales.reshape(pool_dev * 2, heads_kv))
-    regrouped = exchange(by_head, "mp", heads)
-    regrouped = regrouped.reshape(group_rows, slot_rows, DH)
-
+    from_core0 = lax.ppermute(of_core1, "mp", [(2 * y, 2 * y + 1) for y in range(chips)])
+    along_y = exchange(of_core0, "mp", *lists)
     wanted = jnp.take(page_table, fork, axis=0)
     on_device = wanted // group_rows == my_dp
     send_rows = jnp.sum(jnp.where(on_device, wanted % group_rows, 0), axis=1)
-    found = jnp.sum(on_device.astype(jnp.int32), axis=1)
+    sum_rows = (send_rows + (group_rows - heads[0] * pool_dev)) % group_rows
+    sum_rows = jnp.where(jnp.any(on_device, axis=1), sum_rows, group_rows)
+    owner = send_rows // pool_dev
+    chip = (owner // 2 + (chips - first_y)) % chips
+    send_rows = owner % 2 * (group_rows // 2) + chip * pool_dev + send_rows % pool_dev
     sources = jnp.take(wanted, my_dp, axis=0) // group_rows
-    place = jnp.asarray([order.index(d) for d in range(dp_size)], jnp.int32)
+    sources = (sources + (dp_size - order[0])) % dp_size
     send_rows, sum_rows, sources = pl.pallas_call(
-        functools.partial(index_kernel, order, group_rows - heads[0] * pool_dev),
-        out_shape=tuple(pltpu.MemorySpace.SMEM(v.shape, v.dtype) for v in (send_rows, found, sources)),
-        in_specs=[SMEM, SMEM, SMEM, SMEM],
+        functools.partial(index_kernel, order),
+        out_shape=tuple(pltpu.MemorySpace.SMEM(v.shape, v.dtype) for v in (send_rows, sum_rows, sources)),
+        in_specs=[SMEM, SMEM, SMEM],
         out_specs=(SMEM, SMEM, SMEM),
         compiler_params=PARAMS,
-    )(send_rows, found, sources, place)
+    )(send_rows, sum_rows, sources)
 
     own = resp_kv[:, 0]
     rows = jax.ShapeDtypeStruct((q_rows_all, DH), bf16)
     stat = jax.ShapeDtypeStruct((1, q_rows_all), jnp.float32)
+    own_part = jax.ShapeDtypeStruct((resp_len, q_rows_all), jnp.float32)
     q_rows, g_rows, *stats = pl.pallas_call(
         own_kernel,
-        out_shape=(rows, rows, stat, stat, stat),
+        out_shape=(rows, rows, stat, stat, own_part, own_part),
         in_specs=[SMEM, VMEM, VMEM, VMEM],
-        out_specs=(VMEM,) * 5,
+        out_specs=(VMEM,) * 6,
         compiler_params=PARAMS,
         cost_estimate=pl.CostEstimate(flops=10**8, bytes_accessed=2**21, transcendentals=2**17),
     )(lengths, own, resp_q[0], d_out[0])
-    send_rows, q_rows, g_rows = lax.optimization_barrier((send_rows, q_rows, g_rows))
+    along_y, send_rows, q_rows, g_rows = lax.optimization_barrier((along_y, send_rows, q_rows, g_rows))
+    from_core1 = lax.ppermute(along_y, "mp", [(2 * y + 1, 2 * y) for y in range(chips)])
 
     slots = jax.ShapeDtypeStruct((dp_size, slot_rows, DH), bf16)
-    selected = pl.pallas_call(
-        select_kernel,
-        out_shape=slots,
-        in_specs=[SMEM, VMEM],
-        out_specs=VMEM,
-        compiler_params=PARAMS,
-    )(send_rows, regrouped)
-    arrived = exchange(selected, "dp", order)
+
+    def core0(rows, own_pages, other_pages, own_heads, other_heads):
+        selected = pl.pallas_call(
+            select_kernel,
+            out_shape=slots,
+            in_specs=[SMEM, VMEM, VMEM],
+            out_specs=VMEM,
+            compiler_params=PARAMS,
+        )(
+            rows,
+            own_pages.reshape(group_rows // 2, slot_rows, DH),
+            other_pages.reshape(group_rows // 2, slot_rows, DH),
+        )
+        return exchange(selected, "dp", order)
+
+    def core1(rows, own_pages, other_pages, own_heads, other_heads):
+        chip = ((lax.axis_index("mp") // 2 + (chips - first_y)) % chips).reshape(1)
+        parts = pl.pallas_call(
+            pair_kernel,
+            out_shape=(jax.ShapeDtypeStruct((2, stored_rows, DH), bf16),) * chips,
+            in_specs=[SMEM, VMEM, VMEM],
+            out_specs=(VMEM,) * chips,
+            compiler_params=PARAMS,
+        )(chip, other_heads, own_heads)
+        moved = [parts[0]]
+        for d in range(1, chips):
+            pairs = [(2 * y + 1, 2 * ((y + d) % chips) + 1) for y in range(chips)]
+            moved.append(lax.ppermute(parts[d], "mp", pairs))
+        selected = pl.pallas_call(
+            functools.partial(select_chips_kernel, pool_dev),
+            out_shape=slots,
+            in_specs=[SMEM, SMEM] + [VMEM] * chips,
+            out_specs=VMEM,
+            scratch_shapes=[pltpu.VMEM((chips, 2 * pool_dev, slot_rows, DH), bf16)],
+            compiler_params=PARAMS,
+        )(chip, rows, *[v.reshape(2 * pool_dev, slot_rows, DH) for v in moved])
+        return exchange(selected, "dp", order)
+
+    arrived = lax.cond(
+        lax.axis_index("mp") % 2 == 0,
+        core0,
+        core1,
+        send_rows,
+        along_y,
+        from_core1,
+        of_core1,
+        from_core0,
+    )
 
     sent = pl.pallas_call(
         page_grad_kernel,
         out_shape=slots,
-        in_specs=[SMEM] + [VMEM] * 6,
+        in_specs=[SMEM] + [VMEM] * 7,
         out_specs=VMEM,
         scratch_shapes=[pltpu.VMEM((prompt_len, DH), bf16), pltpu.VMEM((prompt_len, DH), bf16)],
         compiler_params=PARAMS,

time: 118 us -> 110 us (0.932)
  blocking collectives: 78.2 us -> 58.4 us
  starting transfers between devices: 18.3 us -> 29.5 us
    all_to_all x2, blocking collectives: 78.2 us -> 58.4 us  [exchange(): lax.all_to_all(parts, axis, split_axis=0, concat_axis=0, axis_index_group...]
    ppermute x0 -> x5, starting transfers between devices: none -> 17.5 us  [the longest x3 9.62 us: core1(): moved.append(lax.ppermute(parts[d], 'mp', pairs))]
    all_to_all x2, starting transfers between devices: 18.3 us -> 12 us  [exchange(): lax.all_to_all(parts, axis, split_axis=0, concat_axis=0, axis_index_group...]
    ppermute x0 -> x5, waiting for transfers between devices: none -> 3.71 us  [the longest x3 2.6 us: core1(): moved.append(lax.ppermute(parts[d], 'mp', pairs))]
    all_to_all x2, waiting for transfers between devices: 6.74 us -> 3.74 us  [exchange(): lax.all_to_all(parts, axis, split_axis=0, concat_axis=0, axis_index_group...]
    pallas_call x4 -> x5, Pallas kernels: 3.55 us -> 3.95 us  [the longest x1 2.14 us: per_device(): pl.pallas_call(functools.partial(scale_kernel, chunks, lists), out_shape=...]
  transfers between devices with their start and end apart: 2 -> 7, of which waited for: 2 -> 3; matrix products, arithmetic and copies ran while one was open for 1% -> 1% of each run, Pallas kernels for 4% -> 4%
where the time goes in v4:
time: 110 us
  blocking collectives  58.4 us (53%)
  starting transfers between devices  29.5 us (27%)
  Pallas kernels  11.8 us (11%)
  waiting for transfers between devices  7.45 us (7%)
  between operations  1.52 us (1%)
    all_to_all x2, blocking collectives, exchange(): lax.all_to_all(parts, axis, split_axis=0, concat_axis=0, axis_index_group...  58.4 us
    all_to_all x2, starting transfers between devices, exchange(): lax.all_to_all(parts, axis, split_axis=0, concat_axis=0, axis_index_group...  12 us
    ppermute x3, starting transfers between devices, core1(): moved.append(lax.ppermute(parts[d], 'mp', pairs))  9.62 us
    ppermute x1, starting transfers between devices, per_device(): lax.ppermute(along_y, 'mp', [(2 * y + 1, 2 * y) for y in range(chips)])  6.49 us
    all_to_all x2, waiting for transfers between devices, exchange(): lax.all_to_all(parts, axis, split_axis=0, concat_axis=0, axis_index_group...  3.74 us
    pallas_call x1, Pallas kernels, per_device(): pl.pallas_call(own_grad_kernel, out_shape=(jax.ShapeDtypeStruct(resp_q.sh...  3.4 us
    ppermute x3, waiting for transfers between devices, core1(): moved.append(lax.ppermute(parts[d], 'mp', pairs))  2.6 us
  transfers between devices with their start and end apart: 7, of which 3 were waited for; matrix products, arithmetic and copies ran while one was open for 1% of the time, Pallas kernels for 4%

profile of v4, /device:TPU:1, one launch (start us, length us, event | category | flops | bytes accessed | tf_op | source)
XLA Modules:
  0.0 109.7 jit_solution(8767698345429288357)
XLA Ops:
  0.6 2.1 %shard_map.104 = (bf16[4,256,128]{2,1,0:T(8,128)(2,1)}, bf16[4,256,128]{2,1,0:T(8,128)(2,1)S(1)}) custom-call(bf16[256,1024]{1,0:T(8,128)(2,1)} %bitcast.34, bf16[16,8]{1,0:T(8,128)(2,1)} %bitcast.36), custom_call_target="tpu_custom_call" | custom-call | tf_op jit(solution)/shard_map/pallas_call | solution.py:269
  2.8 7.3 %all-to-all-start.2 = ((bf16[4,256,128]{2,1,0:T(8,128)(2,1)}), bf16[4,256,128]{2,1,0:T(8,128)(2,1)S(1)}, u32[]{:S(2)}, u32[]{:S(2)}) async-start(bf16[4,256,128]{2,1,0:T(8,128)(2,1)} %get-tuple-element.47), calls=%async_computation.2 | async-start | bytes 524288 | tf_op jit(solution)/shard_map/all_to_all | solution.py:239
  10.1 1.4 %collective-permute-start.3 = (bf16[4,256,128]{2,1,0:T(8,128)(2,1)S(1)}, bf16[4,256,128]{2,1,0:T(8,128)(2,1)S(1)}, u32[]{:S(2)}, u32[]{:S(2)}) collective-permute-start(bf16[4,256,128]{2,1,0:T(8,128)(2,1)S(1)} %get-tuple-element.46), channel_id=1, source_target_pairs={{0,1},{2,3},{4,5},{6,7},{8,9},{10,11},{12,13},{14,15},{16,17},{18,... | collective-permute-start | bytes 786440 | tf_op jit(solution)/shard_map/ppermute | solution.py:284
  12.4 0.6 gather_fusion
  13.0 0.2 fusion.14
  13.2 0.1 fusion.2
  13.4 0.7 shard_map.103
  14.1 0.5 shard_map.105
  14.6 6.5 %collective-permute-start.4 = (bf16[4,256,128]{2,1,0:T(8,128)(2,1)S(1)}, bf16[4,256,128]{2,1,0:T(8,128)(2,1)S(1)}, u32[]{:S(2)}, u32[]{:S(2)}) collective-permute-start(bf16[4,256,128]{2,1,0:T(8,128)(2,1)S(1)} %all-to-all-done.2), channel_id=1, source_target_pairs={{1,0},{3,2},{5,4},{7,6},{9,8},{11,10},{13,12},{15,14},{17,16},{19,... | collective-permute-start | bytes 786440 | tf_op jit(solution)/shard_map/ppermute | solution.py:317
  21.1 1.1 %collective-permute-done.4 = bf16[4,256,128]{2,1,0:T(8,128)(2,1)S(1)} collective-permute-done((bf16[4,256,128]{2,1,0:T(8,128)(2,1)S(1)}, bf16[4,256,128]{2,1,0:T(8,128)(2,1)S(1)}, u32[]{:S(2)}, u32[]{:S(2)}) %collective-permute-start.4) | collective-permute-done | bytes 262176 | tf_op jit(solution)/shard_map/ppermute | solution.py:317
  22.2 43.4 %conditional.1 = (bf16[64,32,128]{2,1,0:T(8,128)(2,1)S(1)}) conditional(s32[]{:T(128)} %convert_element_type.3, (bf16[4,256,128]{2,1,0:T(8,128)(2,1)S(1)}, bf16[4,256,128]{2,1,0:T(8,128)(2,1)S(1)}, s32[64]{0:T(128)S(4)}) %tuple.16, (bf16[4,256,128]{2,1,0:T(8,128)(2,1)S(1)}, bf16[4,256,128]{2,1,0:T(8,128)(2,1)S(1)}, s32[64]{0:T(128)S(4)}) %tuple.17), branch_computations={%region_2.3_spmd, %region_3.4_spmd} | conditional | flops 29 | bytes 2621859 | solution.py:358
  22.3 1.9 %collective-permute-start = (bf16[2,256,128]{2,1,0:T(8,128)(2,1)S(1)}, bf16[2,256,128]{2,1,0:T(8,128)(2,1)S(1)}, u32[]{:S(2)}, u32[]{:S(2)}) collective-permute-start(bf16[2,256,128]{2,1,0:T(8,128)(2,1)S(1)} %get-tuple-element.19), channel_id=1, source_target_pairs={{1,3},{3,5},{5,7},{7,1},{9,11},{11,13},{13,15},{15,9},{17,19},{19,... | collective-permute-start | bytes 393224 | tf_op jit(solution)/shard_map/cond/branch_0_fun/ppermute | solution.py:347
  24.2 4.6 %collective-permute-start.1 = (bf16[2,256,128]{2,1,0:T(8,128)(2,1)S(1)}, bf16[2,256,128]{2,1,0:T(8,128)(2,1)S(1)}, u32[]{:S(2)}, u32[]{:S(2)}) collective-permute-start(bf16[2,256,128]{2,1,0:T(8,128)(2,1)S(1)} %get-tuple-element.20), channel_id=1, source_target_pairs={{1,5},{3,7},{5,1},{7,3},{9,13},{11,15},{13,9},{15,11},{17,21},{19,... | collective-permute-start | bytes 393224 | tf_op jit(solution)/shard_map/cond/branch_0_fun/ppermute | solution.py:347
  28.8 3.1 %collective-permute-start.2 = (bf16[2,256,128]{2,1,0:T(8,128)(2,1)S(1)}, bf16[2,256,128]{2,1,0:T(8,128)(2,1)S(1)}, u32[]{:S(2)}, u32[]{:S(2)}) collective-permute-start(bf16[2,256,128]{2,1,0:T(8,128)(2,1)S(1)} %get-tuple-element.21), channel_id=1, source_target_pairs={{1,7},{3,1},{5,3},{7,5},{9,15},{11,9},{13,11},{15,13},{17,23},{19,... | collective-permute-start | bytes 393224 | tf_op jit(solution)/shard_map/cond/branch_0_fun/ppermute | solution.py:347
  31.9 2.6 %collective-permute-done.2 = bf16[2,256,128]{2,1,0:T(8,128)(2,1)S(1)} collective-permute-done((bf16[2,256,128]{2,1,0:T(8,128)(2,1)S(1)}, bf16[2,256,128]{2,1,0:T(8,128)(2,1)S(1)}, u32[]{:S(2)}, u32[]{:S(2)}) %collective-permute-start.2) | collective-permute-done | bytes 131104 | tf_op jit(solution)/shard_map/cond/branch_0_fun/ppermute | solution.py:347
  34.5 0.6 branch_0_fun.3
  35.1 30.5 %all_to_all.23 = bf16[64,32,128]{2,1,0:T(8,128)(2,1)S(1)} all-to-all(bf16[64,32,128]{2,1,0:T(8,128)(2,1)S(1)} %branch_0_fun.3), channel_id=1, replica_groups={{216,224,232,240,248,256,264,272,280,288,296,304,312,320,328,336,344,35..., dimensions={0} | all-to-all | bytes 1048576 | tf_op jit(solution)/shard_map/cond/branch_0_fun/all_to_all | solution.py:239
  65.7 2.1 %shard_map.107 = bf16[64,32,128]{2,1,0:T(8,128)(2,1)S(1)} custom-call(s32[32]{0:T(128)S(4)} %get-tuple-element.45.sources_ref, bf16[64,32,128]{2,1,0:T(8,128)(2,1)S(1)} %get-tuple-element.81.arrived_ref, bf16[1024,128]{1,0:T(8,128)(2,1)S(1)} %get-tuple-element.53.q_ref, bf16[1024,128]{1,0:T(8,128)(2,1)S(1)} %get-tuple-element.54.g_ref, ...), custom_call_target="tpu_custom_call" | custom-call | tf_op jit(solution)/shard_map/pallas_call | solution.py:369
  67.8 27.8 %all_to_all.25.arrived_ref = bf16[64,32,128]{2,1,0:T(8,128)(2,1)S(1)} all-to-all(bf16[64,32,128]{2,1,0:T(8,128)(2,1)S(1)} %shard_map.107), channel_id=1, replica_groups={{216,224,232,240,248,256,264,272,280,288,296,304,312,320,328,336,344,35..., dimensions={0} | all-to-all | bytes 1048576 | tf_op jit(solution)/shard_map/all_to_all | solution.py:239
  95.6 1.2 %shard_map.108 = bf16[64,32,128]{2,1,0:T(8,128)(2,1)} custom-call(s32[64]{0:T(128)S(4)} %get-tuple-element.57.rows_ref, bf16[64,32,128]{2,1,0:T(8,128)(2,1)S(1)} %all_to_all.25.arrived_ref), custom_call_target="tpu_custom_call" | custom-call | tf_op jit(solution)/shard_map/pallas_call | solution.py:392
  96.8 4.7 %all-to-all-start.4 = ((bf16[8,256,128]{2,1,0:T(8,128)(2,1)}), bf16[8,256,128]{2,1,0:T(8,128)(2,1)S(1)}, u32[]{:S(2)}, u32[]{:S(2)}) async-start(bf16[8,256,128]{2,1,0:T(8,128)(2,1)} %bitcast.16), calls=%async_computation.4 | async-start | bytes 1048576 | tf_op jit(solution)/shard_map/all_to_all | solution.py:239
  101.5 3.4 %shard_map.106 = (bf16[128,1024]{1,0:T(8,128)(2,1)}, bf16[2,128,128]{2,1,0:T(8,128)(2,1)}) custom-call(s32[32]{0:T(128)S(4)} %get-tuple-element.45.sources_ref, bf16[64,32,128]{2,1,0:T(8,128)(2,1)S(1)} %get-tuple-element.81.arrived_ref, bf16[2,128,128]{2,1,0:T(8,128)(2,1)S(1)} %bitcast.31, bf16[1024,128]{1,0:T(8,128)(2,1)S(1)} %get-tuple-element.53.q_ref, ...), custom_call_target="tpu_custom_call" | custom-call | flops 2000000000 | bytes 4194304 | tf_op jit(solution)/shard_map/pallas_call | solution.py:379
  104.9 3.7 %all-to-all-done.4.parts_ref = bf16[8,256,128]{2,1,0:T(8,128)(2,1)S(1)} async-done(((bf16[8,256,128]{2,1,0:T(8,128)(2,1)}), bf16[8,256,128]{2,1,0:T(8,128)(2,1)S(1)}, u32[]{:S(2)}, u32[]{:S(2)}) %all-to-all-start.4) | async-done | bytes 524320 | tf_op jit(solution)/shard_map/all_to_all | solution.py:239
  108.6 1.1 shard_map.109
  (21 shorter events, 0.2 us)
Async XLA Ops:
  2.8 8.7 %copy-start.4 = (s32[64]{0:T(128)S(1)}, s32[64]{0:T(128)}, u32[]{:S(2)}) copy-start(s32[64]{0:T(128)} %param.14) | copy-start | bytes 772
  2.8 11.3 %copy-start.2 = (bf16[2,1,128,128]{3,2,1,0:T(8,128)(2,1)S(1)}, bf16[2,1,128,128]{3,2,1,0:T(8,128)(2,1)}, u32[]{:S(2)}) copy-start(bf16[2,1,128,128]{3,2,1,0:T(8,128)(2,1)} %param.11) | copy-start | bytes 196612
  2.8 11.8 %all-to-all-start.2 = ((bf16[4,256,128]{2,1,0:T(8,128)(2,1)}), bf16[4,256,128]{2,1,0:T(8,128)(2,1)S(1)}, u32[]{:S(2)}, u32[]{:S(2)}) async-start(bf16[4,256,128]{2,1,0:T(8,128)(2,1)} %get-tuple-element.47), calls=%async_computation.2 | async-start | bytes 524288 | tf_op jit(solution)/shard_map/all_to_all | solution.py:239
  10.1 2.2 %copy-start.3 = (s32[128,32]{0,1:T(8,128)S(1)}, s32[128,32]{0,1:T(8,128)}, u32[]{:S(2)}) copy-start(s32[128,32]{0,1:T(8,128)} %param.15) | copy-start | bytes 49156
  10.1 11.1 %collective-permute-start.3 = (bf16[4,256,128]{2,1,0:T(8,128)(2,1)S(1)}, bf16[4,256,128]{2,1,0:T(8,128)(2,1)S(1)}, u32[]{:S(2)}, u32[]{:S(2)}) collective-permute-start(bf16[4,256,128]{2,1,0:T(8,128)(2,1)S(1)} %get-tuple-element.46), channel_id=1, source_target_pairs={{0,1},{2,3},{4,5},{6,7},{8,9},{10,11},{12,13},{14,15},{16,17},{18,... | collective-permute-start | bytes 786440 | tf_op jit(solution)/shard_map/ppermute | solution.py:284
  11.5 2.5 %copy-start.1 = (bf16[1,128,1024]{2,1,0:T(8,128)(2,1)S(1)}, bf16[1,128,1024]{2,1,0:T(8,128)(2,1)}, u32[]{:S(2)}) copy-start(bf16[1,128,1024]{2,1,0:T(8,128)(2,1)} %param.12) | copy-start | bytes 786436
  11.5 2.5 %copy-start = (bf16[1,128,1024]{2,1,0:T(8,128)(2,1)S(1)}, bf16[1,128,1024]{2,1,0:T(8,128)(2,1)}, u32[]{:S(2)}) copy-start(bf16[1,128,1024]{2,1,0:T(8,128)(2,1)} %param.10) | copy-start | bytes 786436
  14.6 7.6 %collective-permute-start.4 = (bf16[4,256,128]{2,1,0:T(8,128)(2,1)S(1)}, bf16[4,256,128]{2,1,0:T(8,128)(2,1)S(1)}, u32[]{:S(2)}, u32[]{:S(2)}) collective-permute-start(bf16[4,256,128]{2,1,0:T(8,128)(2,1)S(1)} %all-to-all-done.2), channel_id=1, source_target_pairs={{1,0},{3,2},{5,4},{7,6},{9,8},{11,10},{13,12},{15,14},{17,16},{19,... | collective-permute-start | bytes 786440 | tf_op jit(solution)/shard_map/ppermute | solution.py:317
  22.3 9.6 %collective-permute-start = (bf16[2,256,128]{2,1,0:T(8,128)(2,1)S(1)}, bf16[2,256,128]{2,1,0:T(8,128)(2,1)S(1)}, u32[]{:S(2)}, u32[]{:S(2)}) collective-permute-start(bf16[2,256,128]{2,1,0:T(8,128)(2,1)S(1)} %get-tuple-element.19), channel_id=1, source_target_pairs={{1,3},{3,5},{5,7},{7,1},{9,11},{11,13},{13,15},{15,9},{17,19},{19,... | collective-permute-start | bytes 393224 | tf_op jit(solution)/shard_map/cond/branch_0_fun/ppermute | solution.py:347
  24.2 7.7 %collective-permute-start.1 = (bf16[2,256,128]{2,1,0:T(8,128)(2,1)S(1)}, bf16[2,256,128]{2,1,0:T(8,128)(2,1)S(1)}, u32[]{:S(2)}, u32[]{:S(2)}) collective-permute-start(bf16[2,256,128]{2,1,0:T(8,128)(2,1)S(1)} %get-tuple-element.20), channel_id=1, source_target_pairs={{1,5},{3,7},{5,1},{7,3},{9,13},{11,15},{13,9},{15,11},{17,21},{19,... | collective-permute-start | bytes 393224 | tf_op jit(solution)/shard_map/cond/branch_0_fun/ppermute | solution.py:347
  28.8 5.7 %collective-permute-start.2 = (bf16[2,256,128]{2,1,0:T(8,128)(2,1)S(1)}, bf16[2,256,128]{2,1,0:T(8,128)(2,1)S(1)}, u32[]{:S(2)}, u32[]{:S(2)}) collective-permute-start(bf16[2,256,128]{2,1,0:T(8,128)(2,1)S(1)} %get-tuple-element.21), channel_id=1, source_target_pairs={{1,7},{3,1},{5,3},{7,5},{9,15},{11,9},{13,11},{15,13},{17,23},{19,... | collective-permute-start | bytes 393224 | tf_op jit(solution)/shard_map/cond/branch_0_fun/ppermute | solution.py:347
  96.8 11.8 %all-to-all-start.4 = ((bf16[8,256,128]{2,1,0:T(8,128)(2,1)}), bf16[8,256,128]{2,1,0:T(8,128)(2,1)S(1)}, u32[]{:S(2)}, u32[]{:S(2)}) async-start(bf16[8,256,128]{2,1,0:T(8,128)(2,1)} %bitcast.16), calls=%async_computation.4 | async-start | bytes 1048576 | tf_op jit(solution)/shard_map/all_to_all | solution.py:239

commit v5 on v4

--- a/solution.py
+++ b/solution.py
@@ -82,17 +82,19 @@
 
 
 def select_chips_kernel(pages_dev, chip_ref, rows_ref, *refs):
-    *arrived_refs, out_ref, pages_ref = refs
+    *arrived_refs, out_ref = refs
     chips = len(arrived_refs)
-    for d in range(chips):
-        pages_ref[d] = arrived_refs[d][...]
     half = chips * pages_dev
     for r in range(out_ref.shape[0]):
         row = rows_ref[r]
         core = lax.div(row, half)
         place = lax.rem(row, half)
         back = lax.rem(chip_ref[0] + chips - lax.div(place, pages_dev), chips)
-        out_ref[r] = pages_ref[back, core * pages_dev + lax.rem(place, pages_dev)]
+        at = core * pages_dev + lax.rem(place, pages_dev)
+        page = arrived_refs[0][at]
+        for d in range(1, chips):
+            page = jnp.where(back == d, arrived_refs[d][at], page)
+        out_ref[r] = page
 
 
 def pair_kernel(chip_ref, first_ref, second_ref, *out_refs):
@@ -230,9 +232,19 @@
     out_ref[...] = total_ref[:pages].astype(jnp.bfloat16)
 
 
-def layout_kernel(order, parts_ref, out_ref):
-    for k, j in enumerate(order):
-        out_ref[:, j * DH : (j + 1) * DH] = parts_ref[k].astype(jnp.float32)
+def layout_kernel(order, parts_ref, out_ref, buf, sems):
+    chunks = sems.shape[0]
+    step = buf.shape[0] // chunks
+    copies = []
+    for c in range(chunks):
+        part = slice(c * step, (c + 1) * step)
+        for k, j in enumerate(order):
+            buf[part, j * DH : (j + 1) * DH] = parts_ref[k, part].astype(jnp.float32)
+        rows = pl.ds(c * step, step)
+        copies.append(pltpu.make_async_copy(buf.at[rows], out_ref.at[rows], sems.at[c]))
+        copies[c].start()
+    for copy in copies:
+        copy.wait()
 
 
 def exchange(parts, axis, *groups):
@@ -350,7 +362,6 @@
             out_shape=slots,
             in_specs=[SMEM, SMEM] + [VMEM] * chips,
             out_specs=VMEM,
-            scratch_shapes=[pltpu.VMEM((chips, 2 * pool_dev, slot_rows, DH), bf16)],
             compiler_params=PARAMS,
         )(chip, rows, *[v.reshape(2 * pool_dev, slot_rows, DH) for v in moved])
         return exchange(selected, "dp", order)
@@ -402,7 +413,11 @@
         functools.partial(layout_kernel, heads),
         out_shape=jax.ShapeDtypeStruct((stored_rows, heads_kv * DH), jnp.float32),
         in_specs=[VMEM],
-        out_specs=VMEM,
+        out_specs=HBM,
+        scratch_shapes=[
+            pltpu.VMEM((stored_rows, heads_kv * DH), jnp.float32),
+            pltpu.SemaphoreType.DMA((4,)),
+        ],
         compiler_params=PARAMS,
     )(restored)
     return d_query[None], d_own[:, None], d_pool.reshape(pool_pages.shape)

time: 110 us -> 110 us (level)
  no operation moved by 1% of the time
where the time goes in v5:
time: 110 us
  blocking collectives  58.2 us (53%)
  starting transfers between devices  29.5 us (27%)
  Pallas kernels  11.9 us (11%)
  waiting for transfers between devices  7.45 us (7%)
  between operations  1.52 us (1%)
    all_to_all x2, blocking collectives, exchange(): lax.all_to_all(parts, axis, split_axis=0, concat_axis=0, axis_index_group...  58.2 us
    all_to_all x2, starting transfers between devices, exchange(): lax.all_to_all(parts, axis, split_axis=0, concat_axis=0, axis_index_group...  11.9 us
    ppermute x3, starting transfers between devices, core1(): moved.append(lax.ppermute(parts[d], 'mp', pairs))  9.62 us
    ppermute x1, starting transfers between devices, per_device(): lax.ppermute(along_y, 'mp', [(2 * y + 1, 2 * y) for y in range(chips)])  6.49 us
    all_to_all x2, waiting for transfers between devices, exchange(): lax.all_to_all(parts, axis, split_axis=0, concat_axis=0, axis_index_group...  3.74 us
    pallas_call x1, Pallas kernels, per_device(): pl.pallas_call(own_grad_kernel, out_shape=(jax.ShapeDtypeStruct(resp_q.sh...  3.4 us
    ppermute x3, waiting for transfers between devices, core1(): moved.append(lax.ppermute(parts[d], 'mp', pairs))  2.6 us
  transfers between devices with their start and end apart: 7, of which 3 were waited for; matrix products, arithmetic and copies ran while one was open for 1% of the time, Pallas kernels for 4%

profile of v5, /device:TPU:1, one launch (start us, length us, event | category | flops | bytes accessed | tf_op | source)
XLA Modules:
  0.0 109.7 jit_solution(10354083082384755389)
XLA Ops:
  0.6 2.1 %shard_map.104 = (bf16[4,256,128]{2,1,0:T(8,128)(2,1)}, bf16[4,256,128]{2,1,0:T(8,128)(2,1)S(1)}) custom-call(bf16[256,1024]{1,0:T(8,128)(2,1)} %bitcast.34, bf16[16,8]{1,0:T(8,128)(2,1)} %bitcast.36), custom_call_target="tpu_custom_call" | custom-call | tf_op jit(solution)/shard_map/pallas_call | solution.py:281
  2.8 7.3 %all-to-all-start.2 = ((bf16[4,256,128]{2,1,0:T(8,128)(2,1)}), bf16[4,256,128]{2,1,0:T(8,128)(2,1)S(1)}, u32[]{:S(2)}, u32[]{:S(2)}) async-start(bf16[4,256,128]{2,1,0:T(8,128)(2,1)} %get-tuple-element.47), calls=%async_computation.2 | async-start | bytes 524288 | tf_op jit(solution)/shard_map/all_to_all | solution.py:251
  10.1 1.4 %collective-permute-start.3 = (bf16[4,256,128]{2,1,0:T(8,128)(2,1)S(1)}, bf16[4,256,128]{2,1,0:T(8,128)(2,1)S(1)}, u32[]{:S(2)}, u32[]{:S(2)}) collective-permute-start(bf16[4,256,128]{2,1,0:T(8,128)(2,1)S(1)} %get-tuple-element.46), channel_id=1, source_target_pairs={{0,1},{2,3},{4,5},{6,7},{8,9},{10,11},{12,13},{14,15},{16,17},{18,... | collective-permute-start | bytes 786440 | tf_op jit(solution)/shard_map/ppermute | solution.py:296
  12.4 0.6 gather_fusion
  13.0 0.2 fusion.14
  13.2 0.1 fusion.2
  13.4 0.7 shard_map.103
  14.1 0.5 shard_map.105
  14.6 6.5 %collective-permute-start.4 = (bf16[4,256,128]{2,1,0:T(8,128)(2,1)S(1)}, bf16[4,256,128]{2,1,0:T(8,128)(2,1)S(1)}, u32[]{:S(2)}, u32[]{:S(2)}) collective-permute-start(bf16[4,256,128]{2,1,0:T(8,128)(2,1)S(1)} %all-to-all-done.2), channel_id=1, source_target_pairs={{1,0},{3,2},{5,4},{7,6},{9,8},{11,10},{13,12},{15,14},{17,16},{19,... | collective-permute-start | bytes 786440 | tf_op jit(solution)/shard_map/ppermute | solution.py:329
  21.1 1.1 %collective-permute-done.4 = bf16[4,256,128]{2,1,0:T(8,128)(2,1)S(1)} collective-permute-done((bf16[4,256,128]{2,1,0:T(8,128)(2,1)S(1)}, bf16[4,256,128]{2,1,0:T(8,128)(2,1)S(1)}, u32[]{:S(2)}, u32[]{:S(2)}) %collective-permute-start.4) | collective-permute-done | bytes 262176 | tf_op jit(solution)/shard_map/ppermute | solution.py:329
  22.2 43.5 %conditional.1 = (bf16[64,32,128]{2,1,0:T(8,128)(2,1)S(1)}) conditional(s32[]{:T(128)} %convert_element_type.3, (bf16[4,256,128]{2,1,0:T(8,128)(2,1)S(1)}, bf16[4,256,128]{2,1,0:T(8,128)(2,1)S(1)}, s32[64]{0:T(128)S(4)}) %tuple.16, (bf16[4,256,128]{2,1,0:T(8,128)(2,1)S(1)}, bf16[4,256,128]{2,1,0:T(8,128)(2,1)S(1)}, s32[64]{0:T(128)S(4)}) %tuple.17), branch_computations={%region_2.3_spmd, %region_3.4_spmd} | conditional | flops 29 | bytes 2621859 | solution.py:369
  22.3 1.9 %collective-permute-start = (bf16[2,256,128]{2,1,0:T(8,128)(2,1)S(1)}, bf16[2,256,128]{2,1,0:T(8,128)(2,1)S(1)}, u32[]{:S(2)}, u32[]{:S(2)}) collective-permute-start(bf16[2,256,128]{2,1,0:T(8,128)(2,1)S(1)} %get-tuple-element.19), channel_id=1, source_target_pairs={{1,3},{3,5},{5,7},{7,1},{9,11},{11,13},{13,15},{15,9},{17,19},{19,... | collective-permute-start | bytes 393224 | tf_op jit(solution)/shard_map/cond/branch_0_fun/ppermute | solution.py:359
  24.2 4.6 %collective-permute-start.1 = (bf16[2,256,128]{2,1,0:T(8,128)(2,1)S(1)}, bf16[2,256,128]{2,1,0:T(8,128)(2,1)S(1)}, u32[]{:S(2)}, u32[]{:S(2)}) collective-permute-start(bf16[2,256,128]{2,1,0:T(8,128)(2,1)S(1)} %get-tuple-element.20), channel_id=1, source_target_pairs={{1,5},{3,7},{5,1},{7,3},{9,13},{11,15},{13,9},{15,11},{17,21},{19,... | collective-permute-start | bytes 393224 | tf_op jit(solution)/shard_map/cond/branch_0_fun/ppermute | solution.py:359
  28.8 3.1 %collective-permute-start.2 = (bf16[2,256,128]{2,1,0:T(8,128)(2,1)S(1)}, bf16[2,256,128]{2,1,0:T(8,128)(2,1)S(1)}, u32[]{:S(2)}, u32[]{:S(2)}) collective-permute-start(bf16[2,256,128]{2,1,0:T(8,128)(2,1)S(1)} %get-tuple-element.21), channel_id=1, source_target_pairs={{1,7},{3,1},{5,3},{7,5},{9,15},{11,9},{13,11},{15,13},{17,23},{19,... | collective-permute-start | bytes 393224 | tf_op jit(solution)/shard_map/cond/branch_0_fun/ppermute | solution.py:359
  31.9 2.6 %collective-permute-done.2 = bf16[2,256,128]{2,1,0:T(8,128)(2,1)S(1)} collective-permute-done((bf16[2,256,128]{2,1,0:T(8,128)(2,1)S(1)}, bf16[2,256,128]{2,1,0:T(8,128)(2,1)S(1)}, u32[]{:S(2)}, u32[]{:S(2)}) %collective-permute-start.2) | collective-permute-done | bytes 131104 | tf_op jit(solution)/shard_map/cond/branch_0_fun/ppermute | solution.py:359
  34.5 0.7 branch_0_fun.3
  35.3 30.5 %all_to_all.23 = bf16[64,32,128]{2,1,0:T(8,128)(2,1)S(1)} all-to-all(bf16[64,32,128]{2,1,0:T(8,128)(2,1)S(1)} %branch_0_fun.3), channel_id=1, replica_groups={{216,224,232,240,248,256,264,272,280,288,296,304,312,320,328,336,344,35..., dimensions={0} | all-to-all | bytes 1048576 | tf_op jit(solution)/shard_map/cond/branch_0_fun/all_to_all | solution.py:251
  65.8 2.1 %shard_map.107 = bf16[64,32,128]{2,1,0:T(8,128)(2,1)S(1)} custom-call(s32[32]{0:T(128)S(4)} %get-tuple-element.45.sources_ref, bf16[64,32,128]{2,1,0:T(8,128)(2,1)S(1)} %get-tuple-element.81.arrived_ref, bf16[1024,128]{1,0:T(8,128)(2,1)S(1)} %get-tuple-element.53.q_ref, bf16[1024,128]{1,0:T(8,128)(2,1)S(1)} %get-tuple-element.54.g_ref, ...), custom_call_target="tpu_custom_call" | custom-call | tf_op jit(solution)/shard_map/pallas_call | solution.py:380
  67.9 27.7 %all_to_all.25.arrived_ref = bf16[64,32,128]{2,1,0:T(8,128)(2,1)S(1)} all-to-all(bf16[64,32,128]{2,1,0:T(8,128)(2,1)S(1)} %shard_map.107), channel_id=1, replica_groups={{216,224,232,240,248,256,264,272,280,288,296,304,312,320,328,336,344,35..., dimensions={0} | all-to-all | bytes 1048576 | tf_op jit(solution)/shard_map/all_to_all | solution.py:251
  95.6 1.2 %shard_map.108 = bf16[64,32,128]{2,1,0:T(8,128)(2,1)} custom-call(s32[64]{0:T(128)S(4)} %get-tuple-element.57.rows_ref, bf16[64,32,128]{2,1,0:T(8,128)(2,1)S(1)} %all_to_all.25.arrived_ref), custom_call_target="tpu_custom_call" | custom-call | tf_op jit(solution)/shard_map/pallas_call | solution.py:403
  96.9 4.7 %all-to-all-start.4 = ((bf16[8,256,128]{2,1,0:T(8,128)(2,1)}), bf16[8,256,128]{2,1,0:T(8,128)(2,1)S(1)}, u32[]{:S(2)}, u32[]{:S(2)}) async-start(bf16[8,256,128]{2,1,0:T(8,128)(2,1)} %bitcast.16), calls=%async_computation.4 | async-start | bytes 1048576 | tf_op jit(solution)/shard_map/all_to_all | solution.py:251
  101.5 3.4 %shard_map.106 = (bf16[128,1024]{1,0:T(8,128)(2,1)}, bf16[2,128,128]{2,1,0:T(8,128)(2,1)}) custom-call(s32[32]{0:T(128)S(4)} %get-tuple-element.45.sources_ref, bf16[64,32,128]{2,1,0:T(8,128)(2,1)S(1)} %get-tuple-element.81.arrived_ref, bf16[2,128,128]{2,1,0:T(8,128)(2,1)S(1)} %bitcast.31, bf16[1024,128]{1,0:T(8,128)(2,1)S(1)} %get-tuple-element.53.q_ref, ...), custom_call_target="tpu_custom_call" | custom-call | flops 2000000000 | bytes 4194304 | tf_op jit(solution)/shard_map/pallas_call | solution.py:390
  104.9 3.7 %all-to-all-done.4.parts_ref = bf16[8,256,128]{2,1,0:T(8,128)(2,1)S(1)} async-done(((bf16[8,256,128]{2,1,0:T(8,128)(2,1)}), bf16[8,256,128]{2,1,0:T(8,128)(2,1)S(1)}, u32[]{:S(2)}, u32[]{:S(2)}) %all-to-all-start.4) | async-done | bytes 524320 | tf_op jit(solution)/shard_map/all_to_all | solution.py:251
  108.7 1.0 shard_map.109
  (21 shorter events, 0.2 us)
Async XLA Ops:
  2.8 8.7 %copy-start.4 = (s32[64]{0:T(128)S(1)}, s32[64]{0:T(128)}, u32[]{:S(2)}) copy-start(s32[64]{0:T(128)} %param.14) | copy-start | bytes 772
  2.8 11.3 %copy-start.2 = (bf16[2,1,128,128]{3,2,1,0:T(8,128)(2,1)S(1)}, bf16[2,1,128,128]{3,2,1,0:T(8,128)(2,1)}, u32[]{:S(2)}) copy-start(bf16[2,1,128,128]{3,2,1,0:T(8,128)(2,1)} %param.11) | copy-start | bytes 196612
  2.8 11.8 %all-to-all-start.2 = ((bf16[4,256,128]{2,1,0:T(8,128)(2,1)}), bf16[4,256,128]{2,1,0:T(8,128)(2,1)S(1)}, u32[]{:S(2)}, u32[]{:S(2)}) async-start(bf16[4,256,128]{2,1,0:T(8,128)(2,1)} %get-tuple-element.47), calls=%async_computation.2 | async-start | bytes 524288 | tf_op jit(solution)/shard_map/all_to_all | solution.py:251
  10.1 2.2 %copy-start.3 = (s32[128,32]{0,1:T(8,128)S(1)}, s32[128,32]{0,1:T(8,128)}, u32[]{:S(2)}) copy-start(s32[128,32]{0,1:T(8,128)} %param.15) | copy-start | bytes 49156
  10.1 11.1 %collective-permute-start.3 = (bf16[4,256,128]{2,1,0:T(8,128)(2,1)S(1)}, bf16[4,256,128]{2,1,0:T(8,128)(2,1)S(1)}, u32[]{:S(2)}, u32[]{:S(2)}) collective-permute-start(bf16[4,256,128]{2,1,0:T(8,128)(2,1)S(1)} %get-tuple-element.46), channel_id=1, source_target_pairs={{0,1},{2,3},{4,5},{6,7},{8,9},{10,11},{12,13},{14,15},{16,17},{18,... | collective-permute-start | bytes 786440 | tf_op jit(solution)/shard_map/ppermute | solution.py:296
  11.5 2.5 %copy-start.1 = (bf16[1,128,1024]{2,1,0:T(8,128)(2,1)S(1)}, bf16[1,128,1024]{2,1,0:T(8,128)(2,1)}, u32[]{:S(2)}) copy-start(bf16[1,128,1024]{2,1,0:T(8,128)(2,1)} %param.12) | copy-start | bytes 786436
  11.5 2.5 %copy-start = (bf16[1,128,1024]{2,1,0:T(8,128)(2,1)S(1)}, bf16[1,128,1024]{2,1,0:T(8,128)(2,1)}, u32[]{:S(2)}) copy-start(bf16[1,128,1024]{2,1,0:T(8,128)(2,1)} %param.10) | copy-start | bytes 786436
  14.6 7.6 %collective-permute-start.4 = (bf16[4,256,128]{2,1,0:T(8,128)(2,1)S(1)}, bf16[4,256,128]{2,1,0:T(8,128)(2,1)S(1)}, u32[]{:S(2)}, u32[]{:S(2)}) collective-permute-start(bf16[4,256,128]{2,1,0:T(8,128)(2,1)S(1)} %all-to-all-done.2), channel_id=1, source_target_pairs={{1,0},{3,2},{5,4},{7,6},{9,8},{11,10},{13,12},{15,14},{17,16},{19,... | collective-permute-start | bytes 786440 | tf_op jit(solution)/shard_map/ppermute | solution.py:329
  22.3 9.6 %collective-permute-start = (bf16[2,256,128]{2,1,0:T(8,128)(2,1)S(1)}, bf16[2,256,128]{2,1,0:T(8,128)(2,1)S(1)}, u32[]{:S(2)}, u32[]{:S(2)}) collective-permute-start(bf16[2,256,128]{2,1,0:T(8,128)(2,1)S(1)} %get-tuple-element.19), channel_id=1, source_target_pairs={{1,3},{3,5},{5,7},{7,1},{9,11},{11,13},{13,15},{15,9},{17,19},{19,... | collective-permute-start | bytes 393224 | tf_op jit(solution)/shard_map/cond/branch_0_fun/ppermute | solution.py:359
  24.2 7.7 %collective-permute-start.1 = (bf16[2,256,128]{2,1,0:T(8,128)(2,1)S(1)}, bf16[2,256,128]{2,1,0:T(8,128)(2,1)S(1)}, u32[]{:S(2)}, u32[]{:S(2)}) collective-permute-start(bf16[2,256,128]{2,1,0:T(8,128)(2,1)S(1)} %get-tuple-element.20), channel_id=1, source_target_pairs={{1,5},{3,7},{5,1},{7,3},{9,13},{11,15},{13,9},{15,11},{17,21},{19,... | collective-permute-start | bytes 393224 | tf_op jit(solution)/shard_map/cond/branch_0_fun/ppermute | solution.py:359
  28.8 5.7 %collective-permute-start.2 = (bf16[2,256,128]{2,1,0:T(8,128)(2,1)S(1)}, bf16[2,256,128]{2,1,0:T(8,128)(2,1)S(1)}, u32[]{:S(2)}, u32[]{:S(2)}) collective-permute-start(bf16[2,256,128]{2,1,0:T(8,128)(2,1)S(1)} %get-tuple-element.21), channel_id=1, source_target_pairs={{1,7},{3,1},{5,3},{7,5},{9,15},{11,9},{13,11},{15,13},{17,23},{19,... | collective-permute-start | bytes 393224 | tf_op jit(solution)/shard_map/cond/branch_0_fun/ppermute | solution.py:359
  96.9 11.8 %all-to-all-start.4 = ((bf16[8,256,128]{2,1,0:T(8,128)(2,1)}), bf16[8,256,128]{2,1,0:T(8,128)(2,1)S(1)}, u32[]{:S(2)}, u32[]{:S(2)}) async-start(bf16[8,256,128]{2,1,0:T(8,128)(2,1)} %bitcast.16), calls=%async_computation.4 | async-start | bytes 1048576 | tf_op jit(solution)/shard_map/all_to_all | solution.py:251

commit v6 on v5

--- a/solution.py
+++ b/solution.py
@@ -82,19 +82,17 @@
 
 
 def select_chips_kernel(pages_dev, chip_ref, rows_ref, *refs):
-    *arrived_refs, out_ref = refs
+    *arrived_refs, out_ref, pages_ref = refs
     chips = len(arrived_refs)
+    for d in range(chips):
+        pages_ref[d] = arrived_refs[d][...]
     half = chips * pages_dev
     for r in range(out_ref.shape[0]):
         row = rows_ref[r]
         core = lax.div(row, half)
         place = lax.rem(row, half)
         back = lax.rem(chip_ref[0] + chips - lax.div(place, pages_dev), chips)
-        at = core * pages_dev + lax.rem(place, pages_dev)
-        page = arrived_refs[0][at]
-        for d in range(1, chips):
-            page = jnp.where(back == d, arrived_refs[d][at], page)
-        out_ref[r] = page
+        out_ref[r] = pages_ref[back, core * pages_dev + lax.rem(place, pages_dev)]
 
 
 def pair_kernel(chip_ref, first_ref, second_ref, *out_refs):
@@ -325,8 +323,9 @@
         compiler_params=PARAMS,
         cost_estimate=pl.CostEstimate(flops=10**8, bytes_accessed=2**21, transcendentals=2**17),
     )(lengths, own, resp_q[0], d_out[0])
-    along_y, send_rows, q_rows, g_rows = lax.optimization_barrier((along_y, send_rows, q_rows, g_rows))
+    along_y, send_rows = lax.optimization_barrier((along_y, send_rows))
     from_core1 = lax.ppermute(along_y, "mp", [(2 * y + 1, 2 * y) for y in range(chips)])
+    from_core1, q_rows, g_rows = lax.optimization_barrier((from_core1, q_rows, g_rows))
 
     slots = jax.ShapeDtypeStruct((dp_size, slot_rows, DH), bf16)
 
@@ -362,6 +361,7 @@
             out_shape=slots,
             in_specs=[SMEM, SMEM] + [VMEM] * chips,
             out_specs=VMEM,
+            scratch_shapes=[pltpu.VMEM((chips, 2 * pool_dev, slot_rows, DH), bf16)],
             compiler_params=PARAMS,
         )(chip, rows, *[v.reshape(2 * pool_dev, slot_rows, DH) for v in moved])
         return exchange(selected, "dp", order)

time: 110 us -> 110 us (level)
  starting transfers between devices: 29.5 us -> 31.2 us
  waiting for transfers between devices: 7.45 us -> 6.34 us
    ppermute x1, waiting for transfers between devices: 1.11 us -> 0.01 us  [per_device(): lax.ppermute(along_y, 'mp', [(2 * y + 1, 2 * y) for y in range(chips)])]
  transfers between devices with their start and end apart: 7 -> 7, of which waited for: 3 -> 2; matrix products, arithmetic and copies ran while one was open for 1% -> 1% of each run, Pallas kernels for 4% -> 4%
where the time goes in v6:
time: 110 us
  blocking collectives  57.7 us (52%)
  starting transfers between devices  31.2 us (28%)
  Pallas kernels  11.7 us (11%)
  waiting for transfers between devices  6.34 us (6%)
  between operations  1.47 us (1%)
    all_to_all x2, blocking collectives, exchange(): lax.all_to_all(parts, axis, split_axis=0, concat_axis=0, axis_index_group...  57.7 us
    all_to_all x2, starting transfers between devices, exchange(): lax.all_to_all(parts, axis, split_axis=0, concat_axis=0, axis_index_group...  12.4 us
    ppermute x3, starting transfers between devices, core1(): moved.append(lax.ppermute(parts[d], 'mp', pairs))  10.5 us
    ppermute x1, starting transfers between devices, per_device(): lax.ppermute(along_y, 'mp', [(2 * y + 1, 2 * y) for y in range(chips)])  6.89 us
    all_to_all x2, waiting for transfers between devices, exchange(): lax.all_to_all(parts, axis, split_axis=0, concat_axis=0, axis_index_group...  3.74 us
    pallas_call x1, Pallas kernels, per_device(): pl.pallas_call(own_grad_kernel, out_shape=(jax.ShapeDtypeStruct(resp_q.sh...  3.4 us
    ppermute x3, waiting for transfers between devices, core1(): moved.append(lax.ppermute(parts[d], 'mp', pairs))  2.59 us
  transfers between devices with their start and end apart: 7, of which 2 were waited for; matrix products, arithmetic and copies ran while one was open for 1% of the time, Pallas kernels for 4%

profile of v6, /device:TPU:1, one launch (start us, length us, event | category | flops | bytes accessed | tf_op | source)
XLA Modules:
  0.0 109.7 jit_solution(2289043443626797770)
XLA Ops:
  0.6 2.1 %shard_map.104 = (bf16[4,256,128]{2,1,0:T(8,128)(2,1)}, bf16[4,256,128]{2,1,0:T(8,128)(2,1)S(1)}) custom-call(bf16[256,1024]{1,0:T(8,128)(2,1)} %bitcast.34, bf16[16,8]{1,0:T(8,128)(2,1)} %bitcast.36), custom_call_target="tpu_custom_call" | custom-call | tf_op jit(solution)/shard_map/pallas_call | solution.py:279
  2.8 7.3 %all-to-all-start.2 = ((bf16[4,256,128]{2,1,0:T(8,128)(2,1)}), bf16[4,256,128]{2,1,0:T(8,128)(2,1)S(1)}, u32[]{:S(2)}, u32[]{:S(2)}) async-start(bf16[4,256,128]{2,1,0:T(8,128)(2,1)} %get-tuple-element.48), calls=%async_computation.2 | async-start | bytes 524288 | tf_op jit(solution)/shard_map/all_to_all | solution.py:249
  10.1 1.4 %collective-permute-start.3 = (bf16[4,256,128]{2,1,0:T(8,128)(2,1)S(1)}, bf16[4,256,128]{2,1,0:T(8,128)(2,1)S(1)}, u32[]{:S(2)}, u32[]{:S(2)}) collective-permute-start(bf16[4,256,128]{2,1,0:T(8,128)(2,1)S(1)} %get-tuple-element.47), channel_id=1, source_target_pairs={{0,1},{2,3},{4,5},{6,7},{8,9},{10,11},{12,13},{14,15},{16,17},{18,... | collective-permute-start | bytes 786440 | tf_op jit(solution)/shard_map/ppermute | solution.py:294
  11.6 0.1 copy.11
  11.7 0.6 gather_fusion
  12.3 0.2 fusion.14
  12.5 0.1 fusion.2
  12.7 0.7 shard_map.103
  13.4 6.9 %collective-permute-start.4 = (bf16[4,256,128]{2,1,0:T(8,128)(2,1)S(1)}, bf16[4,256,128]{2,1,0:T(8,128)(2,1)S(1)}, u32[]{:S(2)}, u32[]{:S(2)}) collective-permute-start(bf16[4,256,128]{2,1,0:T(8,128)(2,1)S(1)} %all-to-all-done.2), channel_id=1, source_target_pairs={{1,0},{3,2},{5,4},{7,6},{9,8},{11,10},{13,12},{15,14},{17,16},{19,... | collective-permute-start | bytes 786440 | tf_op jit(solution)/shard_map/ppermute | solution.py:327
  20.9 0.5 shard_map.105
  21.5 44.1 %conditional.1 = (bf16[64,32,128]{2,1,0:T(8,128)(2,1)S(1)}) conditional(s32[]{:T(128)} %convert_element_type.3, (bf16[4,256,128]{2,1,0:T(8,128)(2,1)S(1)}, bf16[4,256,128]{2,1,0:T(8,128)(2,1)S(1)}, s32[64]{0:T(128)S(4)}) %tuple.17, (bf16[4,256,128]{2,1,0:T(8,128)(2,1)S(1)}, bf16[4,256,128]{2,1,0:T(8,128)(2,1)S(1)}, s32[64]{0:T(128)S(4)}) %tuple.19), branch_computations={%region_2.3_spmd, %region_3.4_spmd} | conditional | flops 29 | bytes 2621859 | solution.py:369
  21.6 2.5 %collective-permute-start = (bf16[2,256,128]{2,1,0:T(8,128)(2,1)S(1)}, bf16[2,256,128]{2,1,0:T(8,128)(2,1)S(1)}, u32[]{:S(2)}, u32[]{:S(2)}) collective-permute-start(bf16[2,256,128]{2,1,0:T(8,128)(2,1)S(1)} %get-tuple-element.19), channel_id=1, source_target_pairs={{1,3},{3,5},{5,7},{7,1},{9,11},{11,13},{13,15},{15,9},{17,19},{19,... | collective-permute-start | bytes 393224 | tf_op jit(solution)/shard_map/cond/branch_0_fun/ppermute | solution.py:358
  24.1 4.9 %collective-permute-start.1 = (bf16[2,256,128]{2,1,0:T(8,128)(2,1)S(1)}, bf16[2,256,128]{2,1,0:T(8,128)(2,1)S(1)}, u32[]{:S(2)}, u32[]{:S(2)}) collective-permute-start(bf16[2,256,128]{2,1,0:T(8,128)(2,1)S(1)} %get-tuple-element.20), channel_id=1, source_target_pairs={{1,5},{3,7},{5,1},{7,3},{9,13},{11,15},{13,9},{15,11},{17,21},{19,... | collective-permute-start | bytes 393224 | tf_op jit(solution)/shard_map/cond/branch_0_fun/ppermute | solution.py:358
  29.0 3.1 %collective-permute-start.2 = (bf16[2,256,128]{2,1,0:T(8,128)(2,1)S(1)}, bf16[2,256,128]{2,1,0:T(8,128)(2,1)S(1)}, u32[]{:S(2)}, u32[]{:S(2)}) collective-permute-start(bf16[2,256,128]{2,1,0:T(8,128)(2,1)S(1)} %get-tuple-element.21), channel_id=1, source_target_pairs={{1,7},{3,1},{5,3},{7,5},{9,15},{11,9},{13,11},{15,13},{17,23},{19,... | collective-permute-start | bytes 393224 | tf_op jit(solution)/shard_map/cond/branch_0_fun/ppermute | solution.py:358
  32.1 2.6 %collective-permute-done.2 = bf16[2,256,128]{2,1,0:T(8,128)(2,1)S(1)} collective-permute-done((bf16[2,256,128]{2,1,0:T(8,128)(2,1)S(1)}, bf16[2,256,128]{2,1,0:T(8,128)(2,1)S(1)}, u32[]{:S(2)}, u32[]{:S(2)}) %collective-permute-start.2) | collective-permute-done | bytes 131104 | tf_op jit(solution)/shard_map/cond/branch_0_fun/ppermute | solution.py:358
  34.7 0.6 branch_0_fun.3
  35.3 30.3 %all_to_all.23 = bf16[64,32,128]{2,1,0:T(8,128)(2,1)S(1)} all-to-all(bf16[64,32,128]{2,1,0:T(8,128)(2,1)S(1)} %branch_0_fun.3), channel_id=1, replica_groups={{216,224,232,240,248,256,264,272,280,288,296,304,312,320,328,336,344,35..., dimensions={0} | all-to-all | bytes 1048576 | tf_op jit(solution)/shard_map/cond/branch_0_fun/all_to_all | solution.py:249
  65.6 2.1 %shard_map.107 = bf16[64,32,128]{2,1,0:T(8,128)(2,1)S(1)} custom-call(s32[32]{0:T(128)S(4)} %get-tuple-element.46.sources_ref, bf16[64,32,128]{2,1,0:T(8,128)(2,1)S(1)} %get-tuple-element.83.arrived_ref, bf16[1024,128]{1,0:T(8,128)(2,1)S(1)} %get-tuple-element.55.q_ref, bf16[1024,128]{1,0:T(8,128)(2,1)S(1)} %get-tuple-element.56.g_ref, ...), custom_call_target="tpu_custom_call" | custom-call | tf_op jit(solution)/shard_map/pallas_call | solution.py:380
  67.7 27.4 %all_to_all.25.arrived_ref = bf16[64,32,128]{2,1,0:T(8,128)(2,1)S(1)} all-to-all(bf16[64,32,128]{2,1,0:T(8,128)(2,1)S(1)} %shard_map.107), channel_id=1, replica_groups={{216,224,232,240,248,256,264,272,280,288,296,304,312,320,328,336,344,35..., dimensions={0} | all-to-all | bytes 1048576 | tf_op jit(solution)/shard_map/all_to_all | solution.py:249
  95.1 1.2 %shard_map.108 = bf16[64,32,128]{2,1,0:T(8,128)(2,1)} custom-call(s32[64]{0:T(128)S(4)} %get-tuple-element.59.rows_ref, bf16[64,32,128]{2,1,0:T(8,128)(2,1)S(1)} %all_to_all.25.arrived_ref), custom_call_target="tpu_custom_call" | custom-call | tf_op jit(solution)/shard_map/pallas_call | solution.py:403
  96.4 5.1 %all-to-all-start.4 = ((bf16[8,256,128]{2,1,0:T(8,128)(2,1)}), bf16[8,256,128]{2,1,0:T(8,128)(2,1)S(1)}, u32[]{:S(2)}, u32[]{:S(2)}) async-start(bf16[8,256,128]{2,1,0:T(8,128)(2,1)} %bitcast.16), calls=%async_computation.4 | async-start | bytes 1048576 | tf_op jit(solution)/shard_map/all_to_all | solution.py:249
  101.5 3.4 %shard_map.106 = (bf16[128,1024]{1,0:T(8,128)(2,1)}, bf16[2,128,128]{2,1,0:T(8,128)(2,1)}) custom-call(s32[32]{0:T(128)S(4)} %get-tuple-element.46.sources_ref, bf16[64,32,128]{2,1,0:T(8,128)(2,1)S(1)} %get-tuple-element.83.arrived_ref, bf16[2,128,128]{2,1,0:T(8,128)(2,1)S(1)} %bitcast.31, bf16[1024,128]{1,0:T(8,128)(2,1)S(1)} %get-tuple-element.55.q_ref, ...), custom_call_target="tpu_custom_call" | custom-call | flops 2000000000 | bytes 4194304 | tf_op jit(solution)/shard_map/pallas_call | solution.py:390
  104.9 3.7 %all-to-all-done.4.parts_ref = bf16[8,256,128]{2,1,0:T(8,128)(2,1)S(1)} async-done(((bf16[8,256,128]{2,1,0:T(8,128)(2,1)}), bf16[8,256,128]{2,1,0:T(8,128)(2,1)S(1)}, u32[]{:S(2)}, u32[]{:S(2)}) %all-to-all-start.4) | async-done | bytes 524320 | tf_op jit(solution)/shard_map/all_to_all | solution.py:249
  108.7 1.0 shard_map.109
  (21 shorter events, 0.2 us)
Async XLA Ops:
  2.8 8.7 %copy-start.4 = (s32[64]{0:T(128)S(1)}, s32[64]{0:T(128)}, u32[]{:S(2)}) copy-start(s32[64]{0:T(128)} %param.14) | copy-start | bytes 772
  2.8 18.1 %copy-start.2 = (bf16[2,1,128,128]{3,2,1,0:T(8,128)(2,1)S(1)}, bf16[2,1,128,128]{3,2,1,0:T(8,128)(2,1)}, u32[]{:S(2)}) copy-start(bf16[2,1,128,128]{3,2,1,0:T(8,128)(2,1)} %param.11) | copy-start | bytes 196612
  2.8 10.5 %all-to-all-start.2 = ((bf16[4,256,128]{2,1,0:T(8,128)(2,1)}), bf16[4,256,128]{2,1,0:T(8,128)(2,1)S(1)}, u32[]{:S(2)}, u32[]{:S(2)}) async-start(bf16[4,256,128]{2,1,0:T(8,128)(2,1)} %get-tuple-element.48), calls=%async_computation.2 | async-start | bytes 524288 | tf_op jit(solution)/shard_map/all_to_all | solution.py:249
  10.1 1.5 %copy-start.3 = (s32[128,32]{0,1:T(8,128)S(1)}, s32[128,32]{0,1:T(8,128)}, u32[]{:S(2)}) copy-start(s32[128,32]{0,1:T(8,128)} %param.15) | copy-start | bytes 49156
  10.1 11.4 %collective-permute-start.3 = (bf16[4,256,128]{2,1,0:T(8,128)(2,1)S(1)}, bf16[4,256,128]{2,1,0:T(8,128)(2,1)S(1)}, u32[]{:S(2)}, u32[]{:S(2)}) collective-permute-start(bf16[4,256,128]{2,1,0:T(8,128)(2,1)S(1)} %get-tuple-element.47), channel_id=1, source_target_pairs={{0,1},{2,3},{4,5},{6,7},{8,9},{10,11},{12,13},{14,15},{16,17},{18,... | collective-permute-start | bytes 786440 | tf_op jit(solution)/shard_map/ppermute | solution.py:294
  11.6 9.4 %copy-start = (bf16[1,128,1024]{2,1,0:T(8,128)(2,1)S(1)}, bf16[1,128,1024]{2,1,0:T(8,128)(2,1)}, u32[]{:S(2)}) copy-start(bf16[1,128,1024]{2,1,0:T(8,128)(2,1)} %param.10) | copy-start | bytes 786436
  11.6 9.4 %copy-start.1 = (bf16[1,128,1024]{2,1,0:T(8,128)(2,1)S(1)}, bf16[1,128,1024]{2,1,0:T(8,128)(2,1)}, u32[]{:S(2)}) copy-start(bf16[1,128,1024]{2,1,0:T(8,128)(2,1)} %param.12) | copy-start | bytes 786436
  13.4 8.1 %collective-permute-start.4 = (bf16[4,256,128]{2,1,0:T(8,128)(2,1)S(1)}, bf16[4,256,128]{2,1,0:T(8,128)(2,1)S(1)}, u32[]{:S(2)}, u32[]{:S(2)}) collective-permute-start(bf16[4,256,128]{2,1,0:T(8,128)(2,1)S(1)} %all-to-all-done.2), channel_id=1, source_target_pairs={{1,0},{3,2},{5,4},{7,6},{9,8},{11,10},{13,12},{15,14},{17,16},{19,... | collective-permute-start | bytes 786440 | tf_op jit(solution)/shard_map/ppermute | solution.py:327
  21.6 10.5 %collective-permute-start = (bf16[2,256,128]{2,1,0:T(8,128)(2,1)S(1)}, bf16[2,256,128]{2,1,0:T(8,128)(2,1)S(1)}, u32[]{:S(2)}, u32[]{:S(2)}) collective-permute-start(bf16[2,256,128]{2,1,0:T(8,128)(2,1)S(1)} %get-tuple-element.19), channel_id=1, source_target_pairs={{1,3},{3,5},{5,7},{7,1},{9,11},{11,13},{13,15},{15,9},{17,19},{19,... | collective-permute-start | bytes 393224 | tf_op jit(solution)/shard_map/cond/branch_0_fun/ppermute | solution.py:358
  24.1 8.0 %collective-permute-start.1 = (bf16[2,256,128]{2,1,0:T(8,128)(2,1)S(1)}, bf16[2,256,128]{2,1,0:T(8,128)(2,1)S(1)}, u32[]{:S(2)}, u32[]{:S(2)}) collective-permute-start(bf16[2,256,128]{2,1,0:T(8,128)(2,1)S(1)} %get-tuple-element.20), channel_id=1, source_target_pairs={{1,5},{3,7},{5,1},{7,3},{9,13},{11,15},{13,9},{15,11},{17,21},{19,... | collective-permute-start | bytes 393224 | tf_op jit(solution)/shard_map/cond/branch_0_fun/ppermute | solution.py:358
  29.0 5.7 %collective-permute-start.2 = (bf16[2,256,128]{2,1,0:T(8,128)(2,1)S(1)}, bf16[2,256,128]{2,1,0:T(8,128)(2,1)S(1)}, u32[]{:S(2)}, u32[]{:S(2)}) collective-permute-start(bf16[2,256,128]{2,1,0:T(8,128)(2,1)S(1)} %get-tuple-element.21), channel_id=1, source_target_pairs={{1,7},{3,1},{5,3},{7,5},{9,15},{11,9},{13,11},{15,13},{17,23},{19,... | collective-permute-start | bytes 393224 | tf_op jit(solution)/shard_map/cond/branch_0_fun/ppermute | solution.py:358
  96.4 12.3 %all-to-all-start.4 = ((bf16[8,256,128]{2,1,0:T(8,128)(2,1)}), bf16[8,256,128]{2,1,0:T(8,128)(2,1)S(1)}, u32[]{:S(2)}, u32[]{:S(2)}) async-start(bf16[8,256,128]{2,1,0:T(8,128)(2,1)} %bitcast.16), calls=%async_computation.4 | async-start | bytes 1048576 | tf_op jit(solution)/shard_map/all_to_all | solution.py:249
